TPU v7x, 512 devices: a whole 4x8x8 slice. The times are simulated.
512 devices in a mesh: seq: 64 (over z, y), head: 8 (over x, core).
Axes of the slice: x: 4, y: 8, z: 8, core: 2. Of those that a mesh axis runs over, the one named last changes fastest.
Arguments:
- queries: bfloat16 [24576, 5120], P(('seq', 'head')), may hold values from -30 to 30
- keys: bfloat16 [24576, 5120], P(('seq', 'head')), may hold values from -30 to 30
- values: bfloat16 [24576, 5120], P(('seq', 'head')), may hold values from -6 to 6
- routes: int32 [192, 3], replicated, may hold values from 0 to 191, as said below
- shot_pairs: int32 [24, 2], replicated, may hold values from 0 to 7, as said below
Outputs:
- attention: bfloat16 [24576, 5120], P(('seq', 'head'))
Inputs may be any that keep to these rules, and one draw needn't show every extreme that they name: `routes`: each query group's list names 3 distinct groups, all held by indices of seq of other shots at the same place within their shot; the query groups of one block name at most 3 groups of any one other block. `shot_pairs`: each row names two different shots.
All inputs are finite; a program needn't handle non-finite values.
Results may differ from a plain program's by a relative error of at most 0.0046.
Values may be sent and summed in bfloat16 or wider, within the bound.
No kernel may reach another device: no remote copies, remote signals or barrier semaphores. Data moves between devices by JAX's collectives and lax.ppermute only.
A program may use at most 64 MiB of HBM per device.

v0:
```python
import jax
import jax.numpy as jnp
from jax import lax
from jax.sharding import PartitionSpec as P

HD = 128
GROUP = 128
SHOT_DEV = 8
ROUTED = 3


def passed_along(value, axis, steps):
    count = lax.axis_size(axis)
    pairs = [(source, (source + steps) % count) for source in range(count)]
    return lax.ppermute(value, axis, pairs)


def pair_table(shot_pairs, shots):
    shot_ids = jnp.arange(shots, dtype=jnp.int32)
    first_match = shot_pairs[:, 0][:, None, None] == shot_ids[None, :, None]
    second_match = shot_pairs[:, 1][:, None, None] == shot_ids[None, None, :]
    linked = jnp.any(first_match & second_match, axis=0)
    return linked | linked.T


def attend(query_block, key_block, value_block, far_key_rows, far_value_rows, allowed):
    tokens_here, features = query_block.shape
    per_block = tokens_here // GROUP
    heads_here = features // HD
    score_scale = 1.0 / HD**0.5
    query_heads = query_block.reshape(tokens_here, heads_here, HD)
    local_keys = key_block.reshape(tokens_here, heads_here, HD)
    local_values = value_block.reshape(tokens_here, heads_here, HD)
    far_keys = far_key_rows.reshape(per_block, ROUTED * GROUP, heads_here, HD)
    far_values = far_value_rows.reshape(per_block, ROUTED * GROUP, heads_here, HD)
    local_scores = (
        jnp.einsum("thd,shd->hts", query_heads, local_keys, preferred_element_type=jnp.float32)
        * score_scale
    )
    query_groups = query_heads.reshape(per_block, GROUP, heads_here, HD)
    far_scores = (
        jnp.einsum("cqhd,ckhd->hcqk", query_groups, far_keys, preferred_element_type=jnp.float32)
        * score_scale
    )
    reachable = jnp.repeat(allowed, GROUP, axis=1)
    far_scores = jnp.where(reachable[None, :, None, :], far_scores, jnp.float32(-1e30))
    row_max = jnp.maximum(
        jnp.max(local_scores, axis=-1),
        jnp.max(far_scores, axis=-1).reshape(heads_here, tokens_here),
    )
    local_weights = jnp.exp(local_scores - row_max[:, :, None])
    far_weights = jnp.exp(far_scores - row_max.reshape(heads_here, per_block, GROUP)[..., None])
    totals = jnp.sum(local_weights, axis=-1) + jnp.sum(far_weights, axis=-1).reshape(
        heads_here, tokens_here
    )
    numerator = jnp.einsum(
        "hts,shd->thd",
        local_weights.astype(jnp.bfloat16),
        local_values,
        preferred_element_type=jnp.float32,
    )
    far_part = jnp.einsum(
        "hcqk,ckhd->cqhd",
        far_weights.astype(jnp.bfloat16),
        far_values,
        preferred_element_type=jnp.float32,
    )
    numerator = numerator + far_part.reshape(tokens_here, heads_here, HD)
    result = numerator / totals.T[:, :, None]
    return result.reshape(tokens_here, features).astype(jnp.bfloat16)


def shards(queries, keys, values, routes, shot_pairs):
    query_block, key_block, value_block = (
        lax.all_to_all(queries, "head", split_axis=1, concat_axis=0, tiled=True),
        lax.all_to_all(keys, "head", split_axis=1, concat_axis=0, tiled=True),
        lax.all_to_all(values, "head", split_axis=1, concat_axis=0, tiled=True),
    )
    tokens_here, features = query_block.shape
    per_block = tokens_here // GROUP
    seq_count = lax.axis_size("seq")
    shots = seq_count // SHOT_DEV
    myself = lax.axis_index("seq")
    my_shot = myself // SHOT_DEV
    my_routes = lax.dynamic_slice_in_dim(routes, myself * per_block, per_block, 0)
    flat_routes = my_routes.reshape(-1)
    source_block = flat_routes // per_block
    source_group = flat_routes % per_block
    far_key_rows = jnp.zeros((per_block * ROUTED, GROUP, features), jnp.bfloat16)
    far_value_rows = jnp.zeros((per_block * ROUTED, GROUP, features), jnp.bfloat16)
    for shot_offset in range(1, shots):
        distance = shot_offset * SHOT_DEV
        sender = (myself - distance) % seq_count
        got_keys, got_values = passed_along((key_block, value_block), "seq", distance)
        got_keys = got_keys.reshape(per_block, GROUP, features)
        got_values = got_values.reshape(per_block, GROUP, features)
        arrived = (source_block == sender)[:, None, None]
        far_key_rows = jnp.where(arrived, jnp.take(got_keys, source_group, axis=0), far_key_rows)
        far_value_rows = jnp.where(
            arrived, jnp.take(got_values, source_group, axis=0), far_value_rows
        )
    linked = pair_table(shot_pairs, shots)
    shot_ids = jnp.arange(shots, dtype=jnp.int32)
    linked_row = jnp.any(linked & (shot_ids == my_shot)[:, None], axis=0)
    route_shots = source_block // SHOT_DEV
    allowed = jnp.any(
        linked_row[None, :] & (route_shots[:, None] == shot_ids[None, :]), axis=1
    ).reshape(per_block, ROUTED)
    result = attend(query_block, key_block, value_block, far_key_rows, far_value_rows, allowed)
    return lax.all_to_all(result, "head", split_axis=0, concat_axis=1, tiled=True)


def solution(mesh):
    return jax.shard_map(
        shards,
        mesh=mesh,
        in_specs=(
            P(("seq", "head"), None),
            P(("seq", "head"), None),
            P(("seq", "head"), None),
            P(),
            P(),
        ),
        out_specs=P(("seq", "head"), None),
        check_vma=False,
    )
```

profile of v0, /device:TPU:1, one launch (start us, length us, event | category | flops | bytes accessed | tf_op | source)
XLA Modules:
  0.0 278.6 jit_solution(2826584986125028264)
XLA Ops:
  1.9 11.0 %all-to-all-start.1 = ((bf16[48,8,640]{2,0,1:T(8,128)(2,1)}), bf16[48,8,640]{2,0,1:T(8,128)(2,1)}, u32[]{:S(2)}, u32[]{:S(2)}) async-start(bf16[48,8,640]{2,0,1:T(8,128)(2,1)} %bitcast.78), calls=%async_computation.1 | async-start | bytes 983040 | tf_op jit(solution)/shard_map/all_to_all | solution.py:76
  14.8 7.4 %all-to-all-done.1 = bf16[48,8,640]{2,0,1:T(8,128)(2,1)} async-done(((bf16[48,8,640]{2,0,1:T(8,128)(2,1)}), bf16[48,8,640]{2,0,1:T(8,128)(2,1)}, u32[]{:S(2)}, u32[]{:S(2)}) %all-to-all-start.1) | async-done | bytes 491552 | tf_op jit(solution)/shard_map/all_to_all | solution.py:76
  22.2 4.9 %all-to-all-start.2 = ((bf16[48,8,640]{2,0,1:T(8,128)(2,1)}), bf16[48,8,640]{2,0,1:T(8,128)(2,1)}, u32[]{:S(2)}, u32[]{:S(2)}) async-start(bf16[48,8,640]{2,0,1:T(8,128)(2,1)} %bitcast.77), calls=%async_computation.2 | async-start | bytes 983040 | tf_op jit(solution)/shard_map/all_to_all | solution.py:77
  27.1 5.6 %collective-permute-start = (bf16[384,640]{1,0:T(8,128)(2,1)}, bf16[384,640]{1,0:T(8,128)(2,1)S(1)}, u32[]{:S(2)}, u32[]{:S(2)}) collective-permute-start(bf16[384,640]{1,0:T(8,128)(2,1)} %bitcast.5), channel_id=1, source_target_pairs={{0,448},{8,456},{16,464},{24,472},{32,480},{40,488},{48,496},{56,5... | collective-permute-start | bytes 1474568 | tf_op jit(solution)/shard_map/ppermute | solution.py:15
  32.6 2.2 collective-permute-start.1
  34.8 1.9 collective-permute-start.2
  37.9 5.4 %all-to-all-start = ((bf16[48,8,640]{2,0,1:T(8,128)(2,1)}), bf16[48,8,640]{2,0,1:T(8,128)(2,1)S(1)}, u32[]{:S(2)}, u32[]{:S(2)}) async-start(bf16[48,8,640]{2,0,1:T(8,128)(2,1)} %bitcast.79), calls=%async_computation | async-start | bytes 983040 | tf_op jit(solution)/shard_map/all_to_all | solution.py:75
  43.4 7.6 %collective-permute-start.3 = (bf16[384,640]{1,0:T(8,128)(2,1)}, bf16[384,640]{1,0:T(8,128)(2,1)}, u32[]{:S(2)}, u32[]{:S(2)}) collective-permute-start(bf16[384,640]{1,0:T(8,128)(2,1)} %bitcast.5), channel_id=1, source_target_pairs={{0,256},{8,264},{16,272},{24,280},{32,288},{40,296},{48,304},{56,3... | collective-permute-start | bytes 1474568 | tf_op jit(solution)/shard_map/ppermute | solution.py:15
  51.0 1.9 collective-permute-start.4
  52.9 3.1 %collective-permute-start.5 = (bf16[384,640]{1,0:T(8,128)(2,1)}, bf16[384,640]{1,0:T(8,128)(2,1)}, u32[]{:S(2)}, u32[]{:S(2)}) collective-permute-start(bf16[384,640]{1,0:T(8,128)(2,1)} %bitcast.5), channel_id=1, source_target_pairs={{0,128},{8,136},{16,144},{24,152},{32,160},{40,168},{48,176},{56,1... | collective-permute-start | bytes 1474568 | tf_op jit(solution)/shard_map/ppermute | solution.py:15
  56.0 7.5 %collective-permute-done.1 = bf16[384,640]{1,0:T(8,128)(2,1)S(1)} collective-permute-done((bf16[384,640]{1,0:T(8,128)(2,1)}, bf16[384,640]{1,0:T(8,128)(2,1)S(1)}, u32[]{:S(2)}, u32[]{:S(2)}) %collective-permute-start.1) | collective-permute-done | bytes 491552 | tf_op jit(solution)/shard_map/ppermute | solution.py:15
  63.5 7.7 %collective-permute-start.6 = (bf16[384,640]{1,0:T(8,128)(2,1)}, bf16[384,640]{1,0:T(8,128)(2,1)}, u32[]{:S(2)}, u32[]{:S(2)}) collective-permute-start(bf16[384,640]{1,0:T(8,128)(2,1)} %bitcast.5), channel_id=1, source_target_pairs={{0,64},{8,72},{16,80},{24,88},{32,96},{40,104},{48,112},{56,120},{... | collective-permute-start | bytes 1474568 | tf_op jit(solution)/shard_map/ppermute | solution.py:15
  71.2 45.9 %collective-permute-done.2 = bf16[384,640]{1,0:T(8,128)(2,1)S(1)} collective-permute-done((bf16[384,640]{1,0:T(8,128)(2,1)}, bf16[384,640]{1,0:T(8,128)(2,1)S(1)}, u32[]{:S(2)}, u32[]{:S(2)}) %collective-permute-start.2) | collective-permute-done | bytes 491552 | tf_op jit(solution)/shard_map/ppermute | solution.py:15
  117.2 1.9 collective-permute-start.7
  122.1 2.4 reshape.273
  124.5 2.0 multiply_reduce_fusion
  126.5 2.4 reshape.284
  128.9 2.0 gather_fusion
  130.9 3.0 %gather_fusion.1 = bf16[9,128,640]{2,1,0:T(8,128)(2,1)} fusion(bf16[3,128,640]{2,1,0:T(8,128)(2,1)} %bitcast.82, s32[1024]{0:T(1024)S(1)} %pad_clamp_fusion), kind=kCustom, calls=%fused_computation.1.clone | custom fusion | bytes 2949156 | tf_op jit(solution)/shard_map/jit(_take)/gather | solution.py:98
  133.9 2.0 gather_fusion.2
  135.9 7.3 %collective-permute-start.8 = (bf16[384,640]{1,0:T(8,128)(2,1)}, bf16[384,640]{1,0:T(8,128)(2,1)S(1)}, u32[]{:S(2)}, u32[]{:S(2)}) collective-permute-start(bf16[384,640]{1,0:T(8,128)(2,1)} %bitcast.17), channel_id=1, source_target_pairs={{0,384},{8,392},{16,400},{24,408},{32,416},{40,424},{48,432},{56,4... | collective-permute-start | bytes 1474568 | tf_op jit(solution)/shard_map/ppermute | solution.py:15
  143.2 3.0 %gather_fusion.3 = bf16[9,128,640]{2,1,0:T(8,128)(2,1)} fusion(bf16[3,128,640]{2,1,0:T(8,128)(2,1)} %bitcast.10, s32[1024]{0:T(1024)S(1)} %pad_clamp_fusion), kind=kCustom, calls=%fused_computation.3.clone | custom fusion | bytes 2949156 | tf_op jit(solution)/shard_map/jit(_take)/gather | solution.py:98
  146.2 1.9 collective-permute-start.9
  148.1 3.0 %gather_fusion.4 = bf16[9,128,640]{2,1,0:T(8,128)(2,1)} fusion(bf16[3,128,640]{2,1,0:T(8,128)(2,1)} %bitcast.11, s32[1024]{0:T(1024)S(1)} %pad_clamp_fusion), kind=kCustom, calls=%fused_computation.4.clone | custom fusion | bytes 2949156 | tf_op jit(solution)/shard_map/jit(_take)/gather | solution.py:98
  151.1 2.2 collective-permute-start.10
  153.2 3.1 %gather_fusion.5 = bf16[9,128,640]{2,1,0:T(8,128)(2,1)} fusion(bf16[3,128,640]{2,1,0:T(8,128)(2,1)} %bitcast.12, s32[1024]{0:T(1024)S(1)} %pad_clamp_fusion), kind=kCustom, calls=%fused_computation.5.clone | custom fusion | bytes 2949156 | tf_op jit(solution)/shard_map/jit(_take)/gather | solution.py:98
  156.3 4.9 %collective-permute-start.11 = (bf16[384,640]{1,0:T(8,128)(2,1)}, bf16[384,640]{1,0:T(8,128)(2,1)}, u32[]{:S(2)}, u32[]{:S(2)}) collective-permute-start(bf16[384,640]{1,0:T(8,128)(2,1)} %bitcast.17), channel_id=1, source_target_pairs={{0,192},{8,200},{16,208},{24,216},{32,224},{40,232},{48,240},{56,2... | collective-permute-start | bytes 1474568 | tf_op jit(solution)/shard_map/ppermute | solution.py:15
  161.2 3.0 %gather_fusion.6 = bf16[9,128,640]{2,1,0:T(8,128)(2,1)} fusion(bf16[3,128,640]{2,1,0:T(8,128)(2,1)} %bitcast.13, s32[1024]{0:T(1024)S(1)} %pad_clamp_fusion), kind=kCustom, calls=%fused_computation.6.clone | custom fusion | bytes 2949156 | tf_op jit(solution)/shard_map/jit(_take)/gather | solution.py:98
  164.2 5.2 %collective-permute-start.12 = (bf16[384,640]{1,0:T(8,128)(2,1)}, bf16[384,640]{1,0:T(8,128)(2,1)}, u32[]{:S(2)}, u32[]{:S(2)}) collective-permute-start(bf16[384,640]{1,0:T(8,128)(2,1)} %bitcast.17), channel_id=1, source_target_pairs={{0,128},{8,136},{16,144},{24,152},{32,160},{40,168},{48,176},{56,1... | collective-permute-start | bytes 1474568 | tf_op jit(solution)/shard_map/ppermute | solution.py:15
  169.4 6.1 %fusion.23 = bf16[9,128,640]{2,1,0:T(8,128)(2,1)} fusion(bf16[9,128,640]{2,1,0:T(8,128)(2,1)} %gather_fusion.6, bf16[9,128,640]{2,1,0:T(8,128)(2,1)} %gather_fusion.5, bf16[9,128,640]{2,1,0:T(8,128)(2,1)} %gather_fusion.4, bf16[9,128,640]{2,1,0:T(8,128)(2,1)} %gather_fusion.3, bf16[9,128,640]{2,1,0:T(8,128)(2,1)} %gather_fusion.2, ...), kind=kLoop, calls=%fused_computation.43 | loop fusion | flops 10321920 | bytes 11796552 | tf_op jit(solution)/shard_map/jit(_where)/select_n | solution.py:98
  175.5 4.3 %reshape.282 = bf16[3,384,5,128]{3,2,1,0:T(8,128)(2,1)} reshape(bf16[9,128,640]{2,1,0:T(8,128)(2,1)} %fusion.23) | data formatting | bytes 2949120 | tf_op jit(solution)/shard_map/reshape | solution.py:34
  179.8 3.0 %gather_fusion.7 = bf16[9,128,640]{2,1,0:T(8,128)(2,1)} fusion(bf16[3,128,640]{2,1,0:T(8,128)(2,1)} %bitcast.18, s32[1024]{0:T(1024)S(1)} %pad_clamp_fusion), kind=kCustom, calls=%fused_computation.7.clone | custom fusion | bytes 2949156 | tf_op jit(solution)/shard_map/jit(_take)/gather | solution.py:100
  182.9 3.8 %collective-permute-done.8 = bf16[384,640]{1,0:T(8,128)(2,1)S(1)} collective-permute-done((bf16[384,640]{1,0:T(8,128)(2,1)}, bf16[384,640]{1,0:T(8,128)(2,1)S(1)}, u32[]{:S(2)}, u32[]{:S(2)}) %collective-permute-start.8) | collective-permute-done | bytes 491552 | tf_op jit(solution)/shard_map/ppermute | solution.py:15
  186.7 2.1 collective-permute-start.13
  188.8 2.0 gather_fusion.8
  190.8 25.6 %collective-permute-done.9 = bf16[384,640]{1,0:T(8,128)(2,1)} collective-permute-done((bf16[384,640]{1,0:T(8,128)(2,1)}, bf16[384,640]{1,0:T(8,128)(2,1)}, u32[]{:S(2)}, u32[]{:S(2)}) %collective-permute-start.9) | collective-permute-done | bytes 491552 | tf_op jit(solution)/shard_map/ppermute | solution.py:15
  216.5 3.0 %gather_fusion.9 = bf16[9,128,640]{2,1,0:T(8,128)(2,1)} fusion(bf16[3,128,640]{2,1,0:T(8,128)(2,1)} %bitcast.21, s32[1024]{0:T(1024)S(1)} %pad_clamp_fusion), kind=kCustom, calls=%fused_computation.9.clone | custom fusion | bytes 2949156 | tf_op jit(solution)/shard_map/jit(_take)/gather | solution.py:100
  219.5 3.0 %gather_fusion.10 = bf16[9,128,640]{2,1,0:T(8,128)(2,1)} fusion(bf16[3,128,640]{2,1,0:T(8,128)(2,1)} %bitcast.22, s32[1024]{0:T(1024)S(1)} %pad_clamp_fusion), kind=kCustom, calls=%fused_computation.10.clone | custom fusion | bytes 2949156 | tf_op jit(solution)/shard_map/jit(_take)/gather | solution.py:100
  222.5 3.0 %gather_fusion.11 = bf16[9,128,640]{2,1,0:T(8,128)(2,1)} fusion(bf16[3,128,640]{2,1,0:T(8,128)(2,1)} %bitcast.23, s32[1024]{0:T(1024)S(1)} %pad_clamp_fusion), kind=kCustom, calls=%fused_computation.11.clone | custom fusion | bytes 2949156 | tf_op jit(solution)/shard_map/jit(_take)/gather | solution.py:100
  225.4 8.2 %collective-permute-done.12 = bf16[384,640]{1,0:T(8,128)(2,1)} collective-permute-done((bf16[384,640]{1,0:T(8,128)(2,1)}, bf16[384,640]{1,0:T(8,128)(2,1)}, u32[]{:S(2)}, u32[]{:S(2)}) %collective-permute-start.12) | collective-permute-done | bytes 491552 | tf_op jit(solution)/shard_map/ppermute | solution.py:15
  233.6 3.0 %gather_fusion.12 = bf16[9,128,640]{2,1,0:T(8,128)(2,1)} fusion(bf16[3,128,640]{2,1,0:T(8,128)(2,1)} %bitcast.24, s32[1024]{0:T(1024)S(1)} %pad_clamp_fusion), kind=kCustom, calls=%fused_computation.12.clone | custom fusion | bytes 2949156 | tf_op jit(solution)/shard_map/jit(_take)/gather | solution.py:100
  236.7 4.3 %bitcast_reduce_fusion = (f32[5,3,128]{2,1,0:T(4,128)S(1)}, f32[5,3,384,128]{3,2,1,0:T(8,128)}) fusion(pred[3,384]{1,0:T(4,128)(4,1)S(1)} %bitcast.94, bf16[3,128,5,128]{3,2,1,0:T(8,128)(2,1)} %reshape_reshape.3, bf16[3,384,5,128]{3,2,1,0:T(8,128)(2,1)} %reshape.282), kind=kOutput, calls=%fused_computation.15 | convolution fusion | flops 190953600 | bytes 4924032 | tf_op jit(solution)/shard_map/cqhd,ckhd->hcqk/dot_general | solution.py:42
  240.9 3.2 %collective-permute-done.13 = bf16[384,640]{1,0:T(8,128)(2,1)} collective-permute-done((bf16[384,640]{1,0:T(8,128)(2,1)}, bf16[384,640]{1,0:T(8,128)(2,1)}, u32[]{:S(2)}, u32[]{:S(2)}) %collective-permute-start.13) | collective-permute-done | bytes 491552 | tf_op jit(solution)/shard_map/ppermute | solution.py:15
  244.1 3.0 %gather_fusion.13 = bf16[9,128,640]{2,1,0:T(8,128)(2,1)} fusion(bf16[3,128,640]{2,1,0:T(8,128)(2,1)} %bitcast.25, s32[1024]{0:T(1024)S(1)} %pad_clamp_fusion), kind=kCustom, calls=%fused_computation.13.clone | custom fusion | bytes 2949156 | tf_op jit(solution)/shard_map/jit(_take)/gather | solution.py:100
  247.1 6.1 %fusion.17 = bf16[9,128,640]{2,1,0:T(8,128)(2,1)} fusion(bf16[9,128,640]{2,1,0:T(8,128)(2,1)} %gather_fusion.13, bf16[9,128,640]{2,1,0:T(8,128)(2,1)} %gather_fusion.12, bf16[9,128,640]{2,1,0:T(8,128)(2,1)} %gather_fusion.11, bf16[9,128,640]{2,1,0:T(8,128)(2,1)} %gather_fusion.10, bf16[9,128,640]{2,1,0:T(8,128)(2,1)} %gather_fusion.9, ...), kind=kLoop, calls=%fused_computation.36 | loop fusion | flops 10321920 | bytes 11796552 | tf_op jit(solution)/shard_map/jit(_where)/select_n | solution.py:99
  253.2 4.3 %reshape.292 = bf16[3,384,5,128]{3,2,1,0:T(8,128)(2,1)} reshape(bf16[9,128,640]{2,1,0:T(8,128)(2,1)} %fusion.17) | data formatting | bytes 2949120 | tf_op jit(solution)/shard_map/reshape | solution.py:35
  257.5 2.8 %fusion.3 = (f32[5,3,128]{2,1,0:T(4,128)S(1)}, bf16[5,3,128,384]{2,3,1,0:T(8,128)(2,1)S(1)}) fusion(f32[5,3,384,128]{3,2,1,0:T(8,128)} %get-tuple-element.26, f32[5,3,128]{2,1,0:T(4,128)S(1)} %max.14, pred[3,384]{1,0:T(4,128)(4,1)S(1)} %bitcast.95), kind=kLoop, calls=%fused_computation.22 | loop fusion | flops 3684480 | bytes 4440192 | tf_op jit(solution)/shard_map/reduce_sum | solution.py:53
  264.2 13.6 %all_to_all.70 = bf16[8,48,640]{2,1,0:T(8,128)(2,1)S(1)} all-to-all(bf16[8,48,640]{2,1,0:T(8,128)(2,1)S(1)} %convert_element_type.16), channel_id=1, replica_groups=mesh['seq'=64,'head'=8] {'head'}, dimensions={0} | all-to-all | bytes 983040 | tf_op jit(solution)/shard_map/all_to_all | solution.py:110
  (65 shorter events, 12.6 us)
Async XLA Ops:
  0.0 12.9 %copy-start.7 = (s32[192,3]{0,1:T(4,128)S(1)}, s32[192,3]{0,1:T(4,128)}, u32[]{:S(2)}) copy-start(s32[192,3]{0,1:T(4,128)} %param.10) | copy-start | bytes 6916
  0.0 13.4 %copy-start.8 = (s32[24,2]{0,1:T(2,128)S(1)}, s32[24,2]{0,1:T(2,128)}, u32[]{:S(2)}) copy-start(s32[24,2]{0,1:T(2,128)} %param.11) | copy-start | bytes 580
  0.0 13.7 %copy-start.5 = (bf16[48,5120]{1,0:T(8,128)(2,1)S(1)}, bf16[48,5120]{1,0:T(8,128)(2,1)}, u32[]{:S(2)}) copy-start(bf16[48,5120]{1,0:T(8,128)(2,1)} %param.9) | copy-start | bytes 1474564
  1.9 35.0 %copy-start.6 = (bf16[48,5120]{1,0:T(8,128)(2,1)S(1)}, bf16[48,5120]{1,0:T(8,128)(2,1)}, u32[]{:S(2)}) copy-start(bf16[48,5120]{1,0:T(8,128)(2,1)} %param.7) | copy-start | bytes 1474564
  1.9 20.3 %all-to-all-start.1 = ((bf16[48,8,640]{2,0,1:T(8,128)(2,1)}), bf16[48,8,640]{2,0,1:T(8,128)(2,1)}, u32[]{:S(2)}, u32[]{:S(2)}) async-start(bf16[48,8,640]{2,0,1:T(8,128)(2,1)} %bitcast.78), calls=%async_computation.1 | async-start | bytes 983040 | tf_op jit(solution)/shard_map/all_to_all | solution.py:76
  22.2 15.7 %all-to-all-start.2 = ((bf16[48,8,640]{2,0,1:T(8,128)(2,1)}), bf16[48,8,640]{2,0,1:T(8,128)(2,1)}, u32[]{:S(2)}, u32[]{:S(2)}) async-start(bf16[48,8,640]{2,0,1:T(8,128)(2,1)} %bitcast.77), calls=%async_computation.2 | async-start | bytes 983040 | tf_op jit(solution)/shard_map/all_to_all | solution.py:77
  27.1 25.9 %collective-permute-start = (bf16[384,640]{1,0:T(8,128)(2,1)}, bf16[384,640]{1,0:T(8,128)(2,1)S(1)}, u32[]{:S(2)}, u32[]{:S(2)}) collective-permute-start(bf16[384,640]{1,0:T(8,128)(2,1)} %bitcast.5), channel_id=1, source_target_pairs={{0,448},{8,456},{16,464},{24,472},{32,480},{40,488},{48,496},{56,5... | collective-permute-start | bytes 1474568 | tf_op jit(solution)/shard_map/ppermute | solution.py:15
  32.6 30.9 %collective-permute-start.1 = (bf16[384,640]{1,0:T(8,128)(2,1)}, bf16[384,640]{1,0:T(8,128)(2,1)S(1)}, u32[]{:S(2)}, u32[]{:S(2)}) collective-permute-start(bf16[384,640]{1,0:T(8,128)(2,1)} %bitcast.5), channel_id=1, source_target_pairs={{0,384},{8,392},{16,400},{24,408},{32,416},{40,424},{48,432},{56,4... | collective-permute-start | bytes 1474568 | tf_op jit(solution)/shard_map/ppermute | solution.py:15
  34.8 82.4 %collective-permute-start.2 = (bf16[384,640]{1,0:T(8,128)(2,1)}, bf16[384,640]{1,0:T(8,128)(2,1)S(1)}, u32[]{:S(2)}, u32[]{:S(2)}) collective-permute-start(bf16[384,640]{1,0:T(8,128)(2,1)} %bitcast.5), channel_id=1, source_target_pairs={{0,320},{8,328},{16,336},{24,344},{32,352},{40,360},{48,368},{56,3... | collective-permute-start | bytes 1474568 | tf_op jit(solution)/shard_map/ppermute | solution.py:15
  37.9 81.3 %all-to-all-start = ((bf16[48,8,640]{2,0,1:T(8,128)(2,1)}), bf16[48,8,640]{2,0,1:T(8,128)(2,1)S(1)}, u32[]{:S(2)}, u32[]{:S(2)}) async-start(bf16[48,8,640]{2,0,1:T(8,128)(2,1)} %bitcast.79), calls=%async_computation | async-start | bytes 983040 | tf_op jit(solution)/shard_map/all_to_all | solution.py:75
  43.4 92.5 %collective-permute-start.3 = (bf16[384,640]{1,0:T(8,128)(2,1)}, bf16[384,640]{1,0:T(8,128)(2,1)}, u32[]{:S(2)}, u32[]{:S(2)}) collective-permute-start(bf16[384,640]{1,0:T(8,128)(2,1)} %bitcast.5), channel_id=1, source_target_pairs={{0,256},{8,264},{16,272},{24,280},{32,288},{40,296},{48,304},{56,3... | collective-permute-start | bytes 1474568 | tf_op jit(solution)/shard_map/ppermute | solution.py:15
  51.0 95.2 %collective-permute-start.4 = (bf16[384,640]{1,0:T(8,128)(2,1)}, bf16[384,640]{1,0:T(8,128)(2,1)}, u32[]{:S(2)}, u32[]{:S(2)}) collective-permute-start(bf16[384,640]{1,0:T(8,128)(2,1)} %bitcast.5), channel_id=1, source_target_pairs={{0,192},{8,200},{16,208},{24,216},{32,224},{40,232},{48,240},{56,2... | collective-permute-start | bytes 1474568 | tf_op jit(solution)/shard_map/ppermute | solution.py:15
  52.9 98.1 %collective-permute-start.5 = (bf16[384,640]{1,0:T(8,128)(2,1)}, bf16[384,640]{1,0:T(8,128)(2,1)}, u32[]{:S(2)}, u32[]{:S(2)}) collective-permute-start(bf16[384,640]{1,0:T(8,128)(2,1)} %bitcast.5), channel_id=1, source_target_pairs={{0,128},{8,136},{16,144},{24,152},{32,160},{40,168},{48,176},{56,1... | collective-permute-start | bytes 1474568 | tf_op jit(solution)/shard_map/ppermute | solution.py:15
  63.5 58.6 %copy-start.1 = (bf16[384,640]{1,0:T(8,128)(2,1)}, bf16[384,640]{1,0:T(8,128)(2,1)S(1)}, u32[]{:S(2)}) copy-start(bf16[384,640]{1,0:T(8,128)(2,1)S(1)} %collective-permute-done.1) | copy-start | bytes 1474564
  63.5 92.8 %collective-permute-start.6 = (bf16[384,640]{1,0:T(8,128)(2,1)}, bf16[384,640]{1,0:T(8,128)(2,1)}, u32[]{:S(2)}, u32[]{:S(2)}) collective-permute-start(bf16[384,640]{1,0:T(8,128)(2,1)} %bitcast.5), channel_id=1, source_target_pairs={{0,64},{8,72},{16,80},{24,88},{32,96},{40,104},{48,112},{56,120},{... | collective-permute-start | bytes 1474568 | tf_op jit(solution)/shard_map/ppermute | solution.py:15
  117.2 5.0 %copy-start.2 = (bf16[384,640]{1,0:T(8,128)(2,1)}, bf16[384,640]{1,0:T(8,128)(2,1)S(1)}, u32[]{:S(2)}) copy-start(bf16[384,640]{1,0:T(8,128)(2,1)S(1)} %collective-permute-done.2) | copy-start | bytes 1474564
  117.2 47.0 %collective-permute-start.7 = (bf16[384,640]{1,0:T(8,128)(2,1)}, bf16[384,640]{1,0:T(8,128)(2,1)}, u32[]{:S(2)}, u32[]{:S(2)}) collective-permute-start(bf16[384,640]{1,0:T(8,128)(2,1)} %bitcast.17), channel_id=1, source_target_pairs={{0,448},{8,456},{16,464},{24,472},{32,480},{40,488},{48,496},{56,5... | collective-permute-start | bytes 1474568 | tf_op jit(solution)/shard_map/ppermute | solution.py:15
  130.8 3.1 %copy-start.3 = (bf16[384,640]{1,0:T(8,128)(2,1)S(1)}, bf16[384,640]{1,0:T(8,128)(2,1)}, u32[]{:S(2)}) copy-start(bf16[384,640]{1,0:T(8,128)(2,1)} %copy-done.2) | copy-start | bytes 1474564
  135.9 50.8 %collective-permute-start.8 = (bf16[384,640]{1,0:T(8,128)(2,1)}, bf16[384,640]{1,0:T(8,128)(2,1)S(1)}, u32[]{:S(2)}, u32[]{:S(2)}) collective-permute-start(bf16[384,640]{1,0:T(8,128)(2,1)} %bitcast.17), channel_id=1, source_target_pairs={{0,384},{8,392},{16,400},{24,408},{32,416},{40,424},{48,432},{56,4... | collective-permute-start | bytes 1474568 | tf_op jit(solution)/shard_map/ppermute | solution.py:15
  146.2 70.3 %collective-permute-start.9 = (bf16[384,640]{1,0:T(8,128)(2,1)}, bf16[384,640]{1,0:T(8,128)(2,1)}, u32[]{:S(2)}, u32[]{:S(2)}) collective-permute-start(bf16[384,640]{1,0:T(8,128)(2,1)} %bitcast.17), channel_id=1, source_target_pairs={{0,320},{8,328},{16,336},{24,344},{32,352},{40,360},{48,368},{56,3... | collective-permute-start | bytes 1474568 | tf_op jit(solution)/shard_map/ppermute | solution.py:15
  151.1 68.4 %collective-permute-start.10 = (bf16[384,640]{1,0:T(8,128)(2,1)}, bf16[384,640]{1,0:T(8,128)(2,1)}, u32[]{:S(2)}, u32[]{:S(2)}) collective-permute-start(bf16[384,640]{1,0:T(8,128)(2,1)} %bitcast.17), channel_id=1, source_target_pairs={{0,256},{8,264},{16,272},{24,280},{32,288},{40,296},{48,304},{56,3... | collective-permute-start | bytes 1474568 | tf_op jit(solution)/shard_map/ppermute | solution.py:15
  156.3 66.1 %collective-permute-start.11 = (bf16[384,640]{1,0:T(8,128)(2,1)}, bf16[384,640]{1,0:T(8,128)(2,1)}, u32[]{:S(2)}, u32[]{:S(2)}) collective-permute-start(bf16[384,640]{1,0:T(8,128)(2,1)} %bitcast.17), channel_id=1, source_target_pairs={{0,192},{8,200},{16,208},{24,216},{32,224},{40,232},{48,240},{56,2... | collective-permute-start | bytes 1474568 | tf_op jit(solution)/shard_map/ppermute | solution.py:15
  164.2 69.4 %collective-permute-start.12 = (bf16[384,640]{1,0:T(8,128)(2,1)}, bf16[384,640]{1,0:T(8,128)(2,1)}, u32[]{:S(2)}, u32[]{:S(2)}) collective-permute-start(bf16[384,640]{1,0:T(8,128)(2,1)} %bitcast.17), channel_id=1, source_target_pairs={{0,128},{8,136},{16,144},{24,152},{32,160},{40,168},{48,176},{56,1... | collective-permute-start | bytes 1474568 | tf_op jit(solution)/shard_map/ppermute | solution.py:15
  186.7 57.4 %collective-permute-start.13 = (bf16[384,640]{1,0:T(8,128)(2,1)}, bf16[384,640]{1,0:T(8,128)(2,1)}, u32[]{:S(2)}, u32[]{:S(2)}) collective-permute-start(bf16[384,640]{1,0:T(8,128)(2,1)} %bitcast.17), channel_id=1, source_target_pairs={{0,64},{8,72},{16,80},{24,88},{32,96},{40,104},{48,112},{56,120},{... | collective-permute-start | bytes 1474568 | tf_op jit(solution)/shard_map/ppermute | solution.py:15
  257.5 2.8 %copy-start = (bf16[3,384,5,128]{3,2,1,0:T(8,128)(2,1)S(1)}, bf16[3,384,5,128]{3,2,1,0:T(8,128)(2,1)}, u32[]{:S(2)}) copy-start(bf16[3,384,5,128]{3,2,1,0:T(8,128)(2,1)} %reshape.292) | copy-start | bytes 4423684
  261.2 1.1 copy-start.4
where the time goes:
time: 280 us; the launch traced here: 279 us
  waiting for transfers between devices  102 us (36%)
  starting transfers between devices  76.6 us (27%)
  local copies, waits for them, and re-layouts  62.3 us (22%)
  other arithmetic  16.1 us (6%)
  blocking collectives  13.6 us (5%)
  matrix products  7.9 us (3%)
    ppermute x14, waiting for transfers between devices, passed_along(): return lax.ppermute(value, axis, pairs)  94.3 us
    ppermute x14, starting transfers between devices, passed_along(): return lax.ppermute(value, axis, pairs)  55.4 us
    gather x7, local copies, waits for them, and re-layouts, shards(): jnp.take(got_values, source_group, axis=0)  20 us
    gather x7, local copies, waits for them, and re-layouts, shards(): jnp.take(got_keys, source_group, axis=0)  19 us
    all_to_all x1, blocking collectives, shards(): lax.all_to_all(result, 'head', split_axis=0, concat_axis=1, tiled=True)  13.6 us
    all_to_all x1, starting transfers between devices, shards(): lax.all_to_all(keys, 'head', split_axis=1, concat_axis=0, tiled=True)  11 us
    all_to_all x1, waiting for transfers between devices, shards(): lax.all_to_all(keys, 'head', split_axis=1, concat_axis=0, tiled=True)  7.43 us
    select_n x1, other arithmetic, shards(): jnp.where(arrived, jnp.take(got_keys, source_group, axis=0), far_key_rows)  6.09 us
  transfers between devices with their start and end apart: 17, of which 7 were waited for; matrix products, arithmetic and copies ran while one was open for 23% of the time, Pallas kernels for 0%

commit v1 on v0

v1 whole, which is shorter than its diff:
```python
import functools

import jax
import jax.numpy as jnp
from jax import lax
from jax.experimental import pallas as pl
from jax.experimental.pallas import tpu as pltpu
from jax.sharding import PartitionSpec as P

HD = 128
GROUP = 128
SHOT_DEV = 8
ROUTED = 3
SHOTS = 8
PER_BLOCK = 3
FAR = PER_BLOCK * ROUTED
HALF = GROUP // 2


def hop(value, axis, shots):
    count = lax.axis_size(axis)
    steps = shots * SHOT_DEV
    pairs = [(source, (source + steps) % count) for source in range(count)]
    return lax.ppermute(value, axis, pairs)


def to_heads(rows):
    tokens, features = rows.shape
    parts = lax.axis_size("head")
    pieces = rows.reshape(tokens, parts, features // parts).transpose(1, 0, 2)
    got = lax.all_to_all(pieces, "head", split_axis=0, concat_axis=0, tiled=True)
    return got.reshape(parts * tokens, features // parts)


def to_tokens(block):
    parts = lax.axis_size("head")
    tokens, features = block.shape
    pieces = block.reshape(parts, tokens // parts, features)
    got = lax.all_to_all(pieces, "head", split_axis=0, concat_axis=0, tiled=True)
    return got.transpose(1, 0, 2).reshape(tokens // parts, parts * features)


def ring(block):
    middle = block.shape[0] // 2
    before, after = [block], [block]
    for _ in range(3):
        before.append(hop(before[-1], "seq", 1))
        after.append(hop(after[-1], "seq", -1))
    upper = hop(before[-1][:middle], "seq", 1)
    lower = hop(after[-1][middle:], "seq", -1)
    return (after[1], after[2], after[3], before[3], before[2], before[1], upper, lower)


def pair_table(shot_pairs, shots):
    shot_ids = jnp.arange(shots, dtype=jnp.int32)
    first_match = shot_pairs[:, 0][:, None, None] == shot_ids[None, :, None]
    second_match = shot_pairs[:, 1][:, None, None] == shot_ids[None, None, :]
    linked = jnp.any(first_match & second_match, axis=0)
    return linked | linked.T


def route_table(routes, shot_pairs):
    myself = lax.axis_index("seq")
    my_shot = myself // SHOT_DEV
    mine = lax.dynamic_slice_in_dim(routes, myself * PER_BLOCK, PER_BLOCK, 0).reshape(-1)
    shot = mine // (PER_BLOCK * SHOT_DEV)
    linked = pair_table(shot_pairs, SHOTS)
    shot_ids = jnp.arange(SHOTS, dtype=jnp.int32)
    row = jnp.any(linked & (shot_ids == my_shot)[:, None], axis=0)
    allowed = jnp.any(row[None, :] & (shot[:, None] == shot_ids[None, :]), axis=1)
    return jnp.concatenate([(shot - my_shot) % SHOTS, mine % PER_BLOCK, allowed.astype(jnp.int32)])


def fetch(table, far, buffer, sem):
    def copy(source, start, slot, at, rows):
        return pltpu.make_async_copy(
            source.at[pl.ds(start, rows), :], buffer.at[slot, pl.ds(at, rows), :], sem
        )

    def one(slot, carry):
        away = table[slot]
        group = table[FAR + slot]
        for place, offset in enumerate((1, 2, 3, 5, 6, 7)):

            @pl.when(away == offset)
            def _(place=place):
                copy(far[place], pl.multiple_of(group * GROUP, GROUP), slot, 0, GROUP).start()

        @pl.when((away == 4) & (group == 0))
        def _():
            copy(far[6], 0, slot, 0, GROUP).start()

        @pl.when((away == 4) & (group == 1))
        def _():
            copy(far[6], GROUP, slot, 0, HALF).start()
            copy(far[7], 0, slot, HALF, HALF).start()

        @pl.when((away == 4) & (group == 2))
        def _():
            copy(far[7], HALF, slot, 0, GROUP).start()

        return carry

    lax.fori_loop(0, FAR, one, 0)
    pltpu.make_async_copy(buffer, buffer, sem).wait()


def score_kernel(table, q_ref, k_ref, *rest):
    far, (w_ref, total_ref, buffer, sem) = rest[:8], rest[8:]
    fetch(table, far, buffer, sem)
    heads = q_ref.shape[1] // HD
    tokens = k_ref.shape[0]
    scale = 1.0 / HD**0.5
    lanes = lax.broadcasted_iota(jnp.int32, (GROUP, HD), 1)
    contract = (((1,), (1,)), ((), ()))
    for c in range(PER_BLOCK):
        rows = slice(c * GROUP, (c + 1) * GROUP)
        totals = jnp.zeros((GROUP, HD), jnp.float32)
        for h in range(heads):
            columns = slice(h * HD, (h + 1) * HD)
            query = q_ref[rows, columns]
            parts = [
                lax.dot_general(
                    query, k_ref[:, columns], contract, preferred_element_type=jnp.float32
                )
                * scale
            ]
            for j in range(ROUTED):
                slot = c * ROUTED + j
                score = lax.dot_general(
                    query, buffer[slot, :, columns], contract, preferred_element_type=jnp.float32
                )
                parts.append(jnp.where(table[2 * FAR + slot] == 1, score * scale, -1e30))
            scores = jnp.concatenate(parts, axis=1)
            weights = jnp.exp(scores - jnp.max(scores, axis=1, keepdims=True))
            total = jnp.sum(weights, axis=1, keepdims=True)
            totals = jnp.where(lanes == h, total, totals)
            w_ref[c * heads + h] = weights.astype(jnp.bfloat16)
        total_ref[c] = totals


def value_kernel(table, w_ref, total_ref, v_ref, *rest):
    far, (o_ref, buffer, sem) = rest[:8], rest[8:]
    fetch(table, far, buffer, sem)
    tokens, features = v_ref.shape
    heads = features // HD
    for c in range(PER_BLOCK):
        rows = slice(c * GROUP, (c + 1) * GROUP)
        for h in range(heads):
            columns = slice(h * HD, (h + 1) * HD)
            weights = w_ref[c * heads + h]
            result = jnp.dot(
                weights[:, :tokens], v_ref[:, columns], preferred_element_type=jnp.float32
            )
            for j in range(ROUTED):
                at = tokens + j * GROUP
                result += jnp.dot(
                    weights[:, at : at + GROUP],
                    buffer[c * ROUTED + j, :, columns],
                    preferred_element_type=jnp.float32,
                )
            o_ref[rows, columns] = (result / total_ref[c][:, h : h + 1]).astype(o_ref.dtype)


VMEM = pl.BlockSpec(memory_space=pltpu.VMEM)
SMEM = pl.BlockSpec(memory_space=pltpu.SMEM)
ANY = pl.BlockSpec(memory_space=pl.ANY)


def kernels(features):
    heads = features // HD
    keys = (PER_BLOCK + ROUTED) * GROUP
    scratch = [pltpu.VMEM((FAR, GROUP, features), jnp.bfloat16), pltpu.SemaphoreType.DMA]
    flops = 2 * PER_BLOCK * GROUP * keys * features
    score = pl.pallas_call(
        score_kernel,
        out_shape=(
            jax.ShapeDtypeStruct((PER_BLOCK * heads, GROUP, keys), jnp.bfloat16),
            jax.ShapeDtypeStruct((PER_BLOCK, GROUP, HD), jnp.float32),
        ),
        in_specs=[SMEM, VMEM, VMEM] + [ANY] * 8,
        out_specs=(VMEM, VMEM),
        scratch_shapes=scratch,
        compiler_params=pltpu.CompilerParams(vmem_limit_bytes=24 << 20),
        cost_estimate=pl.CostEstimate(
            flops=flops, bytes_accessed=6 << 20, transcendentals=flops // HD // 2
        ),
        name="scores",
    )
    value = pl.pallas_call(
        value_kernel,
        out_shape=jax.ShapeDtypeStruct((PER_BLOCK * GROUP, features), jnp.bfloat16),
        in_specs=[SMEM, VMEM, VMEM, VMEM] + [ANY] * 8,
        out_specs=VMEM,
        scratch_shapes=scratch,
        compiler_params=pltpu.CompilerParams(vmem_limit_bytes=24 << 20),
        cost_estimate=pl.CostEstimate(flops=flops, bytes_accessed=6 << 20, transcendentals=0),
        name="weighted_values",
    )
    return score, value


def shards(queries, keys, values, routes, shot_pairs):
    table = route_table(routes, shot_pairs)
    key_block = to_heads(keys)
    value_block = to_heads(values)
    query_block = to_heads(queries)
    score, value = kernels(key_block.shape[1])
    far_keys = ring(key_block)
    weights, totals = score(table, query_block, key_block, *far_keys)
    far_values = ring(value_block)
    return to_tokens(value(table, weights, totals, value_block, *far_values))


def solution(mesh):
    rows = P(("seq", "head"), None)
    return jax.shard_map(
        shards,
        mesh=mesh,
        in_specs=(rows, rows, rows, P(), P()),
        out_specs=rows,
        check_vma=False,
    )
```

time: 280 us -> 133 us (0.47)
  waiting for transfers between devices: 102 us -> 17.1 us
  local copies, waits for them, and re-layouts: 62.3 us -> 14.1 us
  other arithmetic: 16.1 us -> 0.69 us
  Pallas kernels: 0 us -> 8.28 us
  matrix products: 7.9 us -> 0 us
    ppermute x14 -> x16, waiting for transfers between devices: 94.3 us -> 8.76 us  [hop(): return lax.ppermute(value, axis, pairs)]
    gather x14 -> x0, local copies, waits for them, and re-layouts: 39.1 us -> none  [the longest x7 20 us: shards(): jnp.take(got_values, source_group, axis=0)]
    select_n x3 -> x2, other arithmetic: 12.2 us -> 0.02 us  [the longest x1 0.02 us: route_table(): (shot - my_shot) % SHOTS]
    reshape x6 -> x4, local copies, waits for them, and re-layouts: 15 us -> 5.41 us  [the longest x3 4.59 us: to_heads(): pieces = rows.reshape(tokens, parts, features // parts).transpose(1, 0, 2)]
    pallas_call x0 -> x2, Pallas kernels: none -> 8.28 us  [the longest x1 4.95 us: shards(): weights, totals = score(table, query_block, key_block, *far_keys)]
    dot_general x4 -> x0, matrix products: 7.9 us -> none  [the longest x1 4.27 us: attend(): jnp.einsum('cqhd,ckhd->hcqk', query_groups, far_keys, preferred_element_t...]
    unnamed x20 -> x22, local copies, waits for them, and re-layouts: 0.73 us -> 5.18 us
    all_to_all x4 -> x0, local copies, waits for them, and re-layouts: 4.38 us -> none  [the longest x1 1.91 us: shards(): lax.all_to_all(keys, 'head', split_axis=1, concat_axis=0, tiled=True)]
  transfers between devices with their start and end apart: 17 -> 19, of which waited for: 7 -> 5; matrix products, arithmetic and copies ran while one was open for 23% -> 5% of each run, Pallas kernels for 0% -> 4%
where the time goes in v1:
time: 133 us; the launch traced here: 131 us
  starting transfers between devices  74.5 us (56%)
  waiting for transfers between devices  17.1 us (13%)
  blocking collectives  15.7 us (12%)
  local copies, waits for them, and re-layouts  14.1 us (11%)
  Pallas kernels  8.28 us (6%)
    ppermute x16, starting transfers between devices, hop(): return lax.ppermute(value, axis, pairs)  55.5 us
    all_to_all x3, starting transfers between devices, to_heads(): lax.all_to_all(pieces, 'head', split_axis=0, concat_axis=0, tiled=True)  19.1 us
    all_to_all x1, blocking collectives, to_tokens(): lax.all_to_all(pieces, 'head', split_axis=0, concat_axis=0, tiled=True)  15.7 us
    ppermute x16, waiting for transfers between devices, hop(): return lax.ppermute(value, axis, pairs)  8.76 us
    all_to_all x3, waiting for transfers between devices, to_heads(): lax.all_to_all(pieces, 'head', split_axis=0, concat_axis=0, tiled=True)  8.33 us
    unnamed x22, local copies, waits for them, and re-layouts  5.18 us
    pallas_call x1, Pallas kernels, shards(): weights, totals = score(table, query_block, key_block, *far_keys)  4.95 us
    reshape x3, local copies, waits for them, and re-layouts, to_heads(): pieces = rows.reshape(tokens, parts, features // parts).transpose(1, 0, 2)  4.59 us
  transfers between devices with their start and end apart: 19, of which 5 were waited for; matrix products, arithmetic and copies ran while one was open for 5% of the time, Pallas kernels for 4%

profile of v1, /device:TPU:1, one launch (start us, length us, event | category | flops | bytes accessed | tf_op | source)
XLA Modules:
  0.0 130.7 jit_solution(14782553319925638624)
XLA Ops:
  0.0 1.9 %copy.30 = bf16[6,8,8,640]{3,2,0,1:T(8,128)(2,1)} copy(bf16[6,8,8,640]{3,2,1,0:T(8,128)(2,1)} %bitcast.48) | data formatting | bytes 983040 | tf_op jit(solution)/shard_map/reshape | solution.py:30
  1.9 10.3 %all-to-all-start.1 = ((bf16[8,48,640]{2,1,0:T(8,128)(2,1)}), bf16[8,48,640]{2,1,0:T(8,128)(2,1)S(1)}, u32[]{:S(2)}, u32[]{:S(2)}) async-start(bf16[8,48,640]{2,1,0:T(8,128)(2,1)} %bitcast.35), calls=%async_computation.1 | async-start | bytes 983040 | tf_op jit(solution)/shard_map/all_to_all | solution.py:31
  12.2 1.9 %copy.29 = bf16[6,8,8,640]{3,2,0,1:T(8,128)(2,1)} copy(bf16[6,8,8,640]{3,2,1,0:T(8,128)(2,1)} %bitcast.49) | data formatting | bytes 983040 | tf_op jit(solution)/shard_map/reshape | solution.py:30
  14.0 7.3 %all-to-all-done.1 = bf16[8,48,640]{2,1,0:T(8,128)(2,1)S(1)} async-done(((bf16[8,48,640]{2,1,0:T(8,128)(2,1)}), bf16[8,48,640]{2,1,0:T(8,128)(2,1)S(1)}, u32[]{:S(2)}, u32[]{:S(2)}) %all-to-all-start.1) | async-done | bytes 491552 | tf_op jit(solution)/shard_map/all_to_all | solution.py:31
  21.3 4.3 %all-to-all-start.2 = ((bf16[8,48,640]{2,1,0:T(8,128)(2,1)}), bf16[8,48,640]{2,1,0:T(8,128)(2,1)S(1)}, u32[]{:S(2)}, u32[]{:S(2)}) async-start(bf16[8,48,640]{2,1,0:T(8,128)(2,1)} %bitcast.33), calls=%async_computation.2 | async-start | bytes 983040 | tf_op jit(solution)/shard_map/all_to_all | solution.py:31
  25.6 1.9 %collective-permute-start.3 = (bf16[384,640]{1,0:T(8,128)(2,1)S(1)}, bf16[384,640]{1,0:T(8,128)(2,1)S(1)}, u32[]{:S(2)}, u32[]{:S(2)}) collective-permute-start(bf16[384,640]{1,0:T(8,128)(2,1)S(1)} %bitcast.38), channel_id=1, source_target_pairs={{0,64},{8,72},{16,80},{24,88},{32,96},{40,104},{48,112},{56,120},{... | collective-permute-start | bytes 1474568 | tf_op jit(solution)/shard_map/ppermute | solution.py:24
  27.5 6.2 %collective-permute-start = (bf16[384,640]{1,0:T(8,128)(2,1)S(1)}, bf16[384,640]{1,0:T(8,128)(2,1)S(1)}, u32[]{:S(2)}, u32[]{:S(2)}) collective-permute-start(bf16[384,640]{1,0:T(8,128)(2,1)S(1)} %bitcast.39), channel_id=1, source_target_pairs={{0,448},{8,456},{16,464},{24,472},{32,480},{40,488},{48,496},{56,5... | collective-permute-start | bytes 1474568 | tf_op jit(solution)/shard_map/ppermute | solution.py:24
  33.7 1.0 all-to-all-done.2
  34.7 1.9 %collective-permute-start.11 = (bf16[384,640]{1,0:T(8,128)(2,1)S(1)}, bf16[384,640]{1,0:T(8,128)(2,1)S(1)}, u32[]{:S(2)}, u32[]{:S(2)}) collective-permute-start(bf16[384,640]{1,0:T(8,128)(2,1)S(1)} %bitcast.42), channel_id=1, source_target_pairs={{0,64},{8,72},{16,80},{24,88},{32,96},{40,104},{48,112},{56,120},{... | collective-permute-start | bytes 1474568 | tf_op jit(solution)/shard_map/ppermute | solution.py:24
  36.6 6.2 %collective-permute-start.8 = (bf16[384,640]{1,0:T(8,128)(2,1)S(1)}, bf16[384,640]{1,0:T(8,128)(2,1)S(1)}, u32[]{:S(2)}, u32[]{:S(2)}) collective-permute-start(bf16[384,640]{1,0:T(8,128)(2,1)S(1)} %bitcast.43), channel_id=1, source_target_pairs={{0,448},{8,456},{16,464},{24,472},{32,480},{40,488},{48,496},{56,5... | collective-permute-start | bytes 1474568 | tf_op jit(solution)/shard_map/ppermute | solution.py:24
  42.9 0.8 copy.31
  43.7 4.5 %all-to-all-start = ((bf16[8,48,640]{2,1,0:T(8,128)(2,1)}), bf16[8,48,640]{2,1,0:T(8,128)(2,1)S(1)}, u32[]{:S(2)}, u32[]{:S(2)}) async-start(bf16[8,48,640]{2,1,0:T(8,128)(2,1)} %bitcast.46), calls=%async_computation | async-start | bytes 983040 | tf_op jit(solution)/shard_map/all_to_all | solution.py:31
  48.2 1.9 %collective-permute-start.4 = (bf16[384,640]{1,0:T(8,128)(2,1)S(1)}, bf16[384,640]{1,0:T(8,128)(2,1)}, u32[]{:S(2)}, u32[]{:S(2)}) collective-permute-start(bf16[384,640]{1,0:T(8,128)(2,1)S(1)} %collective-permute-done.3.rest_5_), channel_id=1, source_target_pairs={{0,64},{8,72},{16,80},{24,88},{32,96},{40,104},{48,112},{56,120},{... | collective-permute-start | bytes 1474568 | tf_op jit(solution)/shard_map/ppermute | solution.py:24
  50.2 0.8 copy-done
  51.0 4.6 %collective-permute-start.1 = (bf16[384,640]{1,0:T(8,128)(2,1)S(1)}, bf16[384,640]{1,0:T(8,128)(2,1)}, u32[]{:S(2)}, u32[]{:S(2)}) collective-permute-start(bf16[384,640]{1,0:T(8,128)(2,1)S(1)} %collective-permute-done.rest_0_), channel_id=1, source_target_pairs={{0,448},{8,456},{16,464},{24,472},{32,480},{40,488},{48,496},{56,5... | collective-permute-start | bytes 1474568 | tf_op jit(solution)/shard_map/ppermute | solution.py:24
  55.5 0.8 copy-done.2
  56.4 0.1 copy.16
  56.6 1.9 %collective-permute-start.12 = (bf16[384,640]{1,0:T(8,128)(2,1)S(1)}, bf16[384,640]{1,0:T(8,128)(2,1)}, u32[]{:S(2)}, u32[]{:S(2)}) collective-permute-start(bf16[384,640]{1,0:T(8,128)(2,1)S(1)} %collective-permute-done.11.rest_5_), channel_id=1, source_target_pairs={{0,64},{8,72},{16,80},{24,88},{32,96},{40,104},{48,112},{56,120},{... | collective-permute-start | bytes 1474568 | tf_op jit(solution)/shard_map/ppermute | solution.py:24
  58.5 0.8 copy-done.4
  59.3 4.6 %collective-permute-start.9 = (bf16[384,640]{1,0:T(8,128)(2,1)S(1)}, bf16[384,640]{1,0:T(8,128)(2,1)}, u32[]{:S(2)}, u32[]{:S(2)}) collective-permute-start(bf16[384,640]{1,0:T(8,128)(2,1)S(1)} %collective-permute-done.8.rest_0_), channel_id=1, source_target_pairs={{0,448},{8,456},{16,464},{24,472},{32,480},{40,488},{48,496},{56,5... | collective-permute-start | bytes 1474568 | tf_op jit(solution)/shard_map/ppermute | solution.py:24
  63.9 0.8 copy-done.6
  64.7 1.9 %collective-permute-start.5 = (bf16[384,640]{1,0:T(8,128)(2,1)}, bf16[384,640]{1,0:T(8,128)(2,1)S(1)}, u32[]{:S(2)}, u32[]{:S(2)}) collective-permute-start(bf16[384,640]{1,0:T(8,128)(2,1)} %collective-permute-done.4.rest_4_), channel_id=1, source_target_pairs={{0,64},{8,72},{16,80},{24,88},{32,96},{40,104},{48,112},{56,120},{... | collective-permute-start | bytes 1474568 | tf_op jit(solution)/shard_map/ppermute | solution.py:24
  66.6 4.6 %collective-permute-start.2 = (bf16[384,640]{1,0:T(8,128)(2,1)}, bf16[384,640]{1,0:T(8,128)(2,1)S(1)}, u32[]{:S(2)}, u32[]{:S(2)}) collective-permute-start(bf16[384,640]{1,0:T(8,128)(2,1)} %collective-permute-done.1.rest_1_), channel_id=1, source_target_pairs={{0,448},{8,456},{16,464},{24,472},{32,480},{40,488},{48,496},{56,5... | collective-permute-start | bytes 1474568 | tf_op jit(solution)/shard_map/ppermute | solution.py:24
  71.2 0.2 and_reduce_fusion
  71.4 3.3 %collective-permute-done.12.rest_4_ = bf16[384,640]{1,0:T(8,128)(2,1)} collective-permute-done((bf16[384,640]{1,0:T(8,128)(2,1)S(1)}, bf16[384,640]{1,0:T(8,128)(2,1)}, u32[]{:S(2)}, u32[]{:S(2)}) %collective-permute-start.12) | collective-permute-done | bytes 491552 | tf_op jit(solution)/shard_map/ppermute | solution.py:24
  74.7 1.9 %collective-permute-start.13 = (bf16[384,640]{1,0:T(8,128)(2,1)}, bf16[384,640]{1,0:T(8,128)(2,1)S(1)}, u32[]{:S(2)}, u32[]{:S(2)}) collective-permute-start(bf16[384,640]{1,0:T(8,128)(2,1)} %collective-permute-done.12.rest_4_), channel_id=1, source_target_pairs={{0,64},{8,72},{16,80},{24,88},{32,96},{40,104},{48,112},{56,120},{... | collective-permute-start | bytes 1474568 | tf_op jit(solution)/shard_map/ppermute | solution.py:24
  76.6 5.0 %collective-permute-start.10 = (bf16[384,640]{1,0:T(8,128)(2,1)}, bf16[384,640]{1,0:T(8,128)(2,1)S(1)}, u32[]{:S(2)}, u32[]{:S(2)}) collective-permute-start(bf16[384,640]{1,0:T(8,128)(2,1)} %collective-permute-done.9.rest_1_), channel_id=1, source_target_pairs={{0,448},{8,456},{16,464},{24,472},{32,480},{40,488},{48,496},{56,5... | collective-permute-start | bytes 1474568 | tf_op jit(solution)/shard_map/ppermute | solution.py:24
  81.6 0.1 fusion.4
  81.8 0.1 copy.15
  82.0 0.1 copy.14
  82.2 2.9 %collective-permute-done.5.rest_3_ = bf16[384,640]{1,0:T(8,128)(2,1)S(1)} collective-permute-done((bf16[384,640]{1,0:T(8,128)(2,1)}, bf16[384,640]{1,0:T(8,128)(2,1)S(1)}, u32[]{:S(2)}, u32[]{:S(2)}) %collective-permute-start.5) | collective-permute-done | bytes 491552 | tf_op jit(solution)/shard_map/ppermute | solution.py:24
  85.1 0.7 slice.27
  85.8 1.9 %collective-permute-start.6 = (bf16[192,640]{1,0:T(8,128)(2,1)}, bf16[192,640]{1,0:T(8,128)(2,1)}, u32[]{:S(2)}, u32[]{:S(2)}) collective-permute-start(bf16[192,640]{1,0:T(8,128)(2,1)} %slice.27), channel_id=1, source_target_pairs={{0,64},{8,72},{16,80},{24,88},{32,96},{40,104},{48,112},{56,120},{... | collective-permute-start | bytes 737288 | tf_op jit(solution)/shard_map/ppermute | solution.py:24
  87.8 0.7 slice.28
  88.5 4.6 %collective-permute-start.7 = (bf16[192,640]{1,0:T(8,128)(2,1)}, bf16[192,640]{1,0:T(8,128)(2,1)}, u32[]{:S(2)}, u32[]{:S(2)}) collective-permute-start(bf16[192,640]{1,0:T(8,128)(2,1)} %slice.28), channel_id=1, source_target_pairs={{0,448},{8,456},{16,464},{24,472},{32,480},{40,488},{48,496},{56,5... | collective-permute-start | bytes 737288 | tf_op jit(solution)/shard_map/ppermute | solution.py:24
  93.1 0.1 fusion.3
  93.1 2.5 %collective-permute-done.13.rest_3_ = bf16[384,640]{1,0:T(8,128)(2,1)S(1)} collective-permute-done((bf16[384,640]{1,0:T(8,128)(2,1)}, bf16[384,640]{1,0:T(8,128)(2,1)S(1)}, u32[]{:S(2)}, u32[]{:S(2)}) %collective-permute-start.13) | collective-permute-done | bytes 491552 | tf_op jit(solution)/shard_map/ppermute | solution.py:24
  95.7 0.7 slice.29
  96.4 1.9 %collective-permute-start.14 = (bf16[192,640]{1,0:T(8,128)(2,1)}, bf16[192,640]{1,0:T(8,128)(2,1)}, u32[]{:S(2)}, u32[]{:S(2)}) collective-permute-start(bf16[192,640]{1,0:T(8,128)(2,1)} %slice.29), channel_id=1, source_target_pairs={{0,64},{8,72},{16,80},{24,88},{32,96},{40,104},{48,112},{56,120},{... | collective-permute-start | bytes 737288 | tf_op jit(solution)/shard_map/ppermute | solution.py:24
  98.3 0.7 slice.30
  99.0 4.6 %collective-permute-start.15 = (bf16[192,640]{1,0:T(8,128)(2,1)}, bf16[192,640]{1,0:T(8,128)(2,1)}, u32[]{:S(2)}, u32[]{:S(2)}) collective-permute-start(bf16[192,640]{1,0:T(8,128)(2,1)} %slice.30), channel_id=1, source_target_pairs={{0,448},{8,456},{16,464},{24,472},{32,480},{40,488},{48,496},{56,5... | collective-permute-start | bytes 737288 | tf_op jit(solution)/shard_map/ppermute | solution.py:24
  103.6 0.1 fusion.1
  103.8 1.0 copy-done.1
  104.8 1.0 copy-done.3
  105.9 4.9 %scores.1 = (bf16[15,128,768]{2,1,0:T(8,128)(2,1)S(1)}, f32[3,128,128]{2,1,0:T(8,128)S(1)}) custom-call(s32[27]{0:T(128)S(1)} %pad_add_fusion.table, bf16[384,640]{1,0:T(8,128)(2,1)S(1)} %bitcast.41, bf16[384,640]{1,0:T(8,128)(2,1)S(1)} %bitcast.40, bf16[384,640]{1,0:T(8,128)(2,1)S(1)} %copy-done.3, bf16[384,640]{1,0:T(8,128)(2,1)} %collective-permute-done.1.rest_1_, ...), custom_call_target="tpu_custom_call" | custom-call | flops 377487360 | bytes 6291456 | tf_op jit(solution)/shard_map/scores/pallas_call | solution.py:210
  110.9 3.3 %weighted_values.1 = bf16[384,640]{1,0:T(8,128)(2,1)S(1)} custom-call(s32[27]{0:T(128)S(1)} %pad_add_fusion.table, bf16[15,128,768]{2,1,0:T(8,128)(2,1)S(1)} %get-tuple-element.7.w_ref, f32[3,128,128]{2,1,0:T(8,128)S(1)} %get-tuple-element.8.total_ref, bf16[384,640]{1,0:T(8,128)(2,1)S(1)} %bitcast.44, bf16[384,640]{1,0:T(8,128)(2,1)S(1)} %copy-done.7, ...), custom_call_target="tpu_custom_call" | custom-call | flops 377487360 | bytes 6291456 | tf_op jit(solution)/shard_map/weighted_values/pallas_call | solution.py:212
  114.2 15.7 %all_to_all.20 = bf16[8,48,640]{2,1,0:T(8,128)(2,1)S(1)} all-to-all(bf16[8,48,640]{2,1,0:T(8,128)(2,1)S(1)} %bitcast.45), channel_id=1, replica_groups=mesh['seq'=64,'head'=8] {'head'}, dimensions={0} | all-to-all | bytes 983040 | tf_op jit(solution)/shard_map/all_to_all | solution.py:39
  129.9 0.8 copy.25
  (42 shorter events, 0.6 us)
Async XLA Ops:
  0.0 42.8 %copy-start.8 = (bf16[48,5120]{1,0:T(8,128)(2,1)S(1)}, bf16[48,5120]{1,0:T(8,128)(2,1)}, u32[]{:S(2)}) copy-start(bf16[48,5120]{1,0:T(8,128)(2,1)} %param.5) | copy-start | bytes 1474564
  0.0 48.2 %copy-start.10 = (s32[24,2]{0,1:T(2,128)S(1)}, s32[24,2]{0,1:T(2,128)}, u32[]{:S(2)}) copy-start(s32[24,2]{0,1:T(2,128)} %param.9) | copy-start | bytes 580
  0.0 56.3 %copy-start.9 = (s32[192,3]{0,1:T(4,128)S(1)}, s32[192,3]{0,1:T(4,128)}, u32[]{:S(2)}) copy-start(s32[192,3]{0,1:T(4,128)} %param.8) | copy-start | bytes 6916
  1.9 19.4 %all-to-all-start.1 = ((bf16[8,48,640]{2,1,0:T(8,128)(2,1)}), bf16[8,48,640]{2,1,0:T(8,128)(2,1)S(1)}, u32[]{:S(2)}, u32[]{:S(2)}) async-start(bf16[8,48,640]{2,1,0:T(8,128)(2,1)} %bitcast.35), calls=%async_computation.1 | async-start | bytes 983040 | tf_op jit(solution)/shard_map/all_to_all | solution.py:31
  21.3 13.4 %all-to-all-start.2 = ((bf16[8,48,640]{2,1,0:T(8,128)(2,1)}), bf16[8,48,640]{2,1,0:T(8,128)(2,1)S(1)}, u32[]{:S(2)}, u32[]{:S(2)}) async-start(bf16[8,48,640]{2,1,0:T(8,128)(2,1)} %bitcast.33), calls=%async_computation.2 | async-start | bytes 983040 | tf_op jit(solution)/shard_map/all_to_all | solution.py:31
  25.6 22.6 %collective-permute-start.3 = (bf16[384,640]{1,0:T(8,128)(2,1)S(1)}, bf16[384,640]{1,0:T(8,128)(2,1)S(1)}, u32[]{:S(2)}, u32[]{:S(2)}) collective-permute-start(bf16[384,640]{1,0:T(8,128)(2,1)S(1)} %bitcast.38), channel_id=1, source_target_pairs={{0,64},{8,72},{16,80},{24,88},{32,96},{40,104},{48,112},{56,120},{... | collective-permute-start | bytes 1474568 | tf_op jit(solution)/shard_map/ppermute | solution.py:24
  27.5 23.5 %collective-permute-start = (bf16[384,640]{1,0:T(8,128)(2,1)S(1)}, bf16[384,640]{1,0:T(8,128)(2,1)S(1)}, u32[]{:S(2)}, u32[]{:S(2)}) collective-permute-start(bf16[384,640]{1,0:T(8,128)(2,1)S(1)} %bitcast.39), channel_id=1, source_target_pairs={{0,448},{8,456},{16,464},{24,472},{32,480},{40,488},{48,496},{56,5... | collective-permute-start | bytes 1474568 | tf_op jit(solution)/shard_map/ppermute | solution.py:24
  34.7 21.8 %collective-permute-start.11 = (bf16[384,640]{1,0:T(8,128)(2,1)S(1)}, bf16[384,640]{1,0:T(8,128)(2,1)S(1)}, u32[]{:S(2)}, u32[]{:S(2)}) collective-permute-start(bf16[384,640]{1,0:T(8,128)(2,1)S(1)} %bitcast.42), channel_id=1, source_target_pairs={{0,64},{8,72},{16,80},{24,88},{32,96},{40,104},{48,112},{56,120},{... | collective-permute-start | bytes 1474568 | tf_op jit(solution)/shard_map/ppermute | solution.py:24
  36.6 22.6 %collective-permute-start.8 = (bf16[384,640]{1,0:T(8,128)(2,1)S(1)}, bf16[384,640]{1,0:T(8,128)(2,1)S(1)}, u32[]{:S(2)}, u32[]{:S(2)}) collective-permute-start(bf16[384,640]{1,0:T(8,128)(2,1)S(1)} %bitcast.43), channel_id=1, source_target_pairs={{0,448},{8,456},{16,464},{24,472},{32,480},{40,488},{48,496},{56,5... | collective-permute-start | bytes 1474568 | tf_op jit(solution)/shard_map/ppermute | solution.py:24
  43.7 60.1 %all-to-all-start = ((bf16[8,48,640]{2,1,0:T(8,128)(2,1)}), bf16[8,48,640]{2,1,0:T(8,128)(2,1)S(1)}, u32[]{:S(2)}, u32[]{:S(2)}) async-start(bf16[8,48,640]{2,1,0:T(8,128)(2,1)} %bitcast.46), calls=%async_computation | async-start | bytes 983040 | tf_op jit(solution)/shard_map/all_to_all | solution.py:31
  48.2 16.4 %collective-permute-start.4 = (bf16[384,640]{1,0:T(8,128)(2,1)S(1)}, bf16[384,640]{1,0:T(8,128)(2,1)}, u32[]{:S(2)}, u32[]{:S(2)}) collective-permute-start(bf16[384,640]{1,0:T(8,128)(2,1)S(1)} %collective-permute-done.3.rest_5_), channel_id=1, source_target_pairs={{0,64},{8,72},{16,80},{24,88},{32,96},{40,104},{48,112},{56,120},{... | collective-permute-start | bytes 1474568 | tf_op jit(solution)/shard_map/ppermute | solution.py:24
  50.2 0.8 copy-start
  51.0 15.6 %collective-permute-start.1 = (bf16[384,640]{1,0:T(8,128)(2,1)S(1)}, bf16[384,640]{1,0:T(8,128)(2,1)}, u32[]{:S(2)}, u32[]{:S(2)}) collective-permute-start(bf16[384,640]{1,0:T(8,128)(2,1)S(1)} %collective-permute-done.rest_0_), channel_id=1, source_target_pairs={{0,448},{8,456},{16,464},{24,472},{32,480},{40,488},{48,496},{56,5... | collective-permute-start | bytes 1474568 | tf_op jit(solution)/shard_map/ppermute | solution.py:24
  55.5 0.8 copy-start.2
  56.6 18.1 %collective-permute-start.12 = (bf16[384,640]{1,0:T(8,128)(2,1)S(1)}, bf16[384,640]{1,0:T(8,128)(2,1)}, u32[]{:S(2)}, u32[]{:S(2)}) collective-permute-start(bf16[384,640]{1,0:T(8,128)(2,1)S(1)} %collective-permute-done.11.rest_5_), channel_id=1, source_target_pairs={{0,64},{8,72},{16,80},{24,88},{32,96},{40,104},{48,112},{56,120},{... | collective-permute-start | bytes 1474568 | tf_op jit(solution)/shard_map/ppermute | solution.py:24
  58.5 0.8 copy-start.4
  59.3 17.3 %collective-permute-start.9 = (bf16[384,640]{1,0:T(8,128)(2,1)S(1)}, bf16[384,640]{1,0:T(8,128)(2,1)}, u32[]{:S(2)}, u32[]{:S(2)}) collective-permute-start(bf16[384,640]{1,0:T(8,128)(2,1)S(1)} %collective-permute-done.8.rest_0_), channel_id=1, source_target_pairs={{0,448},{8,456},{16,464},{24,472},{32,480},{40,488},{48,496},{56,5... | collective-permute-start | bytes 1474568 | tf_op jit(solution)/shard_map/ppermute | solution.py:24
  63.9 0.8 copy-start.6
  64.7 20.5 %collective-permute-start.5 = (bf16[384,640]{1,0:T(8,128)(2,1)}, bf16[384,640]{1,0:T(8,128)(2,1)S(1)}, u32[]{:S(2)}, u32[]{:S(2)}) collective-permute-start(bf16[384,640]{1,0:T(8,128)(2,1)} %collective-permute-done.4.rest_4_), channel_id=1, source_target_pairs={{0,64},{8,72},{16,80},{24,88},{32,96},{40,104},{48,112},{56,120},{... | collective-permute-start | bytes 1474568 | tf_op jit(solution)/shard_map/ppermute | solution.py:24
  66.6 21.2 %collective-permute-start.2 = (bf16[384,640]{1,0:T(8,128)(2,1)}, bf16[384,640]{1,0:T(8,128)(2,1)S(1)}, u32[]{:S(2)}, u32[]{:S(2)}) collective-permute-start(bf16[384,640]{1,0:T(8,128)(2,1)} %collective-permute-done.1.rest_1_), channel_id=1, source_target_pairs={{0,448},{8,456},{16,464},{24,472},{32,480},{40,488},{48,496},{56,5... | collective-permute-start | bytes 1474568 | tf_op jit(solution)/shard_map/ppermute | solution.py:24
  74.7 21.0 %collective-permute-start.13 = (bf16[384,640]{1,0:T(8,128)(2,1)}, bf16[384,640]{1,0:T(8,128)(2,1)S(1)}, u32[]{:S(2)}, u32[]{:S(2)}) collective-permute-start(bf16[384,640]{1,0:T(8,128)(2,1)} %collective-permute-done.12.rest_4_), channel_id=1, source_target_pairs={{0,64},{8,72},{16,80},{24,88},{32,96},{40,104},{48,112},{56,120},{... | collective-permute-start | bytes 1474568 | tf_op jit(solution)/shard_map/ppermute | solution.py:24
  76.6 21.7 %collective-permute-start.10 = (bf16[384,640]{1,0:T(8,128)(2,1)}, bf16[384,640]{1,0:T(8,128)(2,1)S(1)}, u32[]{:S(2)}, u32[]{:S(2)}) collective-permute-start(bf16[384,640]{1,0:T(8,128)(2,1)} %collective-permute-done.9.rest_1_), channel_id=1, source_target_pairs={{0,448},{8,456},{16,464},{24,472},{32,480},{40,488},{48,496},{56,5... | collective-permute-start | bytes 1474568 | tf_op jit(solution)/shard_map/ppermute | solution.py:24
  85.8 18.0 %collective-permute-start.6 = (bf16[192,640]{1,0:T(8,128)(2,1)}, bf16[192,640]{1,0:T(8,128)(2,1)}, u32[]{:S(2)}, u32[]{:S(2)}) collective-permute-start(bf16[192,640]{1,0:T(8,128)(2,1)} %slice.27), channel_id=1, source_target_pairs={{0,64},{8,72},{16,80},{24,88},{32,96},{40,104},{48,112},{56,120},{... | collective-permute-start | bytes 737288 | tf_op jit(solution)/shard_map/ppermute | solution.py:24
  88.5 15.3 %collective-permute-start.7 = (bf16[192,640]{1,0:T(8,128)(2,1)}, bf16[192,640]{1,0:T(8,128)(2,1)}, u32[]{:S(2)}, u32[]{:S(2)}) collective-permute-start(bf16[192,640]{1,0:T(8,128)(2,1)} %slice.28), channel_id=1, source_target_pairs={{0,448},{8,456},{16,464},{24,472},{32,480},{40,488},{48,496},{56,5... | collective-permute-start | bytes 737288 | tf_op jit(solution)/shard_map/ppermute | solution.py:24
  96.4 14.4 %collective-permute-start.14 = (bf16[192,640]{1,0:T(8,128)(2,1)}, bf16[192,640]{1,0:T(8,128)(2,1)}, u32[]{:S(2)}, u32[]{:S(2)}) collective-permute-start(bf16[192,640]{1,0:T(8,128)(2,1)} %slice.29), channel_id=1, source_target_pairs={{0,64},{8,72},{16,80},{24,88},{32,96},{40,104},{48,112},{56,120},{... | collective-permute-start | bytes 737288 | tf_op jit(solution)/shard_map/ppermute | solution.py:24
  99.0 11.8 %collective-permute-start.15 = (bf16[192,640]{1,0:T(8,128)(2,1)}, bf16[192,640]{1,0:T(8,128)(2,1)}, u32[]{:S(2)}, u32[]{:S(2)}) collective-permute-start(bf16[192,640]{1,0:T(8,128)(2,1)} %slice.30), channel_id=1, source_target_pairs={{0,448},{8,456},{16,464},{24,472},{32,480},{40,488},{48,496},{56,5... | collective-permute-start | bytes 737288 | tf_op jit(solution)/shard_map/ppermute | solution.py:24
  103.8 1.0 copy-start.1
  104.8 1.0 copy-start.3
  105.9 5.0 %copy-start.5 = (bf16[384,640]{1,0:T(8,128)(2,1)S(1)}, bf16[384,640]{1,0:T(8,128)(2,1)}, u32[]{:S(2)}) copy-start(bf16[384,640]{1,0:T(8,128)(2,1)} %copy-done.4) | copy-start | bytes 1474564
  105.9 5.0 %copy-start.7 = (bf16[384,640]{1,0:T(8,128)(2,1)S(1)}, bf16[384,640]{1,0:T(8,128)(2,1)}, u32[]{:S(2)}) copy-start(bf16[384,640]{1,0:T(8,128)(2,1)} %copy-done.6) | copy-start | bytes 1474564

commit v2 on v1

--- a/solution.py
+++ b/solution.py
@@ -40,15 +40,12 @@
     return got.transpose(1, 0, 2).reshape(tokens // parts, parts * features)
 
 
-def ring(block):
-    middle = block.shape[0] // 2
-    before, after = [block], [block]
-    for _ in range(3):
-        before.append(hop(before[-1], "seq", 1))
-        after.append(hop(after[-1], "seq", -1))
-    upper = hop(before[-1][:middle], "seq", 1)
-    lower = hop(after[-1][middle:], "seq", -1)
-    return (after[1], after[2], after[3], before[3], before[2], before[1], upper, lower)
+def after(value, *others):
+    return lax.optimization_barrier((value, *others))[0]
+
+
+def in_hbm(arrays):
+    return [pltpu.with_memory_space_constraint(array, pltpu.HBM) for array in arrays]
 
 
 def pair_table(shot_pairs, shots):
@@ -71,11 +68,13 @@
     return jnp.concatenate([(shot - my_shot) % SHOTS, mine % PER_BLOCK, allowed.astype(jnp.int32)])
 
 
-def fetch(table, far, buffer, sem):
+def fetch(table, far, buffer, sems):
     def copy(source, start, slot, at, rows):
-        return pltpu.make_async_copy(
-            source.at[pl.ds(start, rows), :], buffer.at[slot, pl.ds(at, rows), :], sem
-        )
+        pltpu.make_async_copy(
+            source.at[pl.ds(start, rows), :],
+            buffer.at[slot, pl.ds(at, rows), :],
+            sems.at[slot // ROUTED],
+        ).start()
 
     def one(slot, carry):
         away = table[slot]
@@ -84,36 +83,41 @@
 
             @pl.when(away == offset)
             def _(place=place):
-                copy(far[place], pl.multiple_of(group * GROUP, GROUP), slot, 0, GROUP).start()
+                copy(far[place], pl.multiple_of(group * GROUP, GROUP), slot, 0, GROUP)
 
         @pl.when((away == 4) & (group == 0))
         def _():
-            copy(far[6], 0, slot, 0, GROUP).start()
+            copy(far[6], 0, slot, 0, GROUP)
 
         @pl.when((away == 4) & (group == 1))
         def _():
-            copy(far[6], GROUP, slot, 0, HALF).start()
-            copy(far[7], 0, slot, HALF, HALF).start()
+            copy(far[6], GROUP, slot, 0, HALF)
+            copy(far[7], 0, slot, HALF, HALF)
 
         @pl.when((away == 4) & (group == 2))
         def _():
-            copy(far[7], HALF, slot, 0, GROUP).start()
+            copy(far[7], HALF, slot, 0, GROUP)
 
         return carry
 
     lax.fori_loop(0, FAR, one, 0)
-    pltpu.make_async_copy(buffer, buffer, sem).wait()
+
+
+def arrived(buffer, sems, c):
+    slots = buffer.at[pl.ds(c * ROUTED, ROUTED)]
+    pltpu.make_async_copy(slots, slots, sems.at[c]).wait()
 
 
 def score_kernel(table, q_ref, k_ref, *rest):
-    far, (w_ref, total_ref, buffer, sem) = rest[:8], rest[8:]
-    fetch(table, far, buffer, sem)
+    far, (w_ref, total_ref, buffer, sems) = rest[:8], rest[8:]
+    fetch(table, far, buffer, sems)
     heads = q_ref.shape[1] // HD
     tokens = k_ref.shape[0]
     scale = 1.0 / HD**0.5
     lanes = lax.broadcasted_iota(jnp.int32, (GROUP, HD), 1)
     contract = (((1,), (1,)), ((), ()))
     for c in range(PER_BLOCK):
+        arrived(buffer, sems, c)
         rows = slice(c * GROUP, (c + 1) * GROUP)
         totals = jnp.zeros((GROUP, HD), jnp.float32)
         for h in range(heads):
@@ -140,11 +144,12 @@
 
 
 def value_kernel(table, w_ref, total_ref, v_ref, *rest):
-    far, (o_ref, buffer, sem) = rest[:8], rest[8:]
-    fetch(table, far, buffer, sem)
+    far, (o_ref, buffer, sems) = rest[:8], rest[8:]
+    fetch(table, far, buffer, sems)
     tokens, features = v_ref.shape
     heads = features // HD
     for c in range(PER_BLOCK):
+        arrived(buffer, sems, c)
         rows = slice(c * GROUP, (c + 1) * GROUP)
         for h in range(heads):
             columns = slice(h * HD, (h + 1) * HD)
@@ -170,7 +175,7 @@
 def kernels(features):
     heads = features // HD
     keys = (PER_BLOCK + ROUTED) * GROUP
-    scratch = [pltpu.VMEM((FAR, GROUP, features), jnp.bfloat16), pltpu.SemaphoreType.DMA]
+    scratch = [pltpu.VMEM((FAR, GROUP, features), jnp.bfloat16), pltpu.SemaphoreType.DMA((PER_BLOCK,))]
     flops = 2 * PER_BLOCK * GROUP * keys * features
     score = pl.pallas_call(
         score_kernel,
@@ -202,13 +207,25 @@
 
 def shards(queries, keys, values, routes, shot_pairs):
     table = route_table(routes, shot_pairs)
+    up = functools.partial(hop, axis="seq", shots=1)
+    down = functools.partial(hop, axis="seq", shots=-1)
     key_block = to_heads(keys)
     value_block = to_heads(values)
     query_block = to_heads(queries)
+    k_up1, k_down1 = up(key_block), down(key_block)
+    v_up1, v_down1 = up(value_block), down(value_block)
+    k_up2, k_down2 = up(k_up1), down(k_down1)
+    v_up2, v_down2 = up(v_up1), down(v_down1)
+    k_up3, k_down3 = up(k_up2), down(k_down2)
+    v_up3, v_down3 = up(v_up2), down(v_down2)
+    middle = key_block.shape[0] // 2
+    k_upper, k_lower = up(k_up3[:middle]), down(k_down3[middle:])
+    v_upper, v_lower = up(v_up3[:middle]), down(v_down3[middle:])
     score, value = kernels(key_block.shape[1])
-    far_keys = ring(key_block)
+    far_keys = (k_down1, k_down2, k_down3, k_up3, k_up2, k_up1, k_upper, k_lower)
+    far_values = (v_down1, v_down2, v_down3, v_up3, v_up2, v_up1, v_upper, v_lower)
+    far_keys, far_values = in_hbm(far_keys), in_hbm(far_values)
     weights, totals = score(table, query_block, key_block, *far_keys)
-    far_values = ring(value_block)
     return to_tokens(value(table, weights, totals, value_block, *far_values))
 
 

time: 133 us -> 129 us (0.970); the launches traced: 131 us -> 128 us
  local copies, waits for them, and re-layouts: 14.1 us -> 9.17 us
  waiting for transfers between devices: 17.1 us -> 20.4 us
    unnamed x22, local copies, waits for them, and re-layouts: 5.18 us -> 0.04 us
    ppermute x16, waiting for transfers between devices: 8.76 us -> 12.1 us  [hop(): return lax.ppermute(value, axis, pairs)]
  transfers between devices with their start and end apart: 19 -> 19, of which waited for: 5 -> 6; matrix products, arithmetic and copies ran while one was open for 5% -> 6% of each run, Pallas kernels for 4% -> 4%
where the time goes in v2:
time: 129 us; the launch traced here: 128 us
  starting transfers between devices  74.1 us (57%)
  waiting for transfers between devices  20.4 us (16%)
  blocking collectives  15.6 us (12%)
  local copies, waits for them, and re-layouts  9.17 us (7%)
  Pallas kernels  7.84 us (6%)
    ppermute x16, starting transfers between devices, hop(): return lax.ppermute(value, axis, pairs)  55.1 us
    all_to_all x3, starting transfers between devices, to_heads(): lax.all_to_all(pieces, 'head', split_axis=0, concat_axis=0, tiled=True)  19.1 us
    all_to_all x1, blocking collectives, to_tokens(): lax.all_to_all(pieces, 'head', split_axis=0, concat_axis=0, tiled=True)  15.6 us
    ppermute x16, waiting for transfers between devices, hop(): return lax.ppermute(value, axis, pairs)  12.1 us
    all_to_all x3, waiting for transfers between devices, to_heads(): lax.all_to_all(pieces, 'head', split_axis=0, concat_axis=0, tiled=True)  8.33 us
    pallas_call x1, Pallas kernels, shards(): weights, totals = score(table, query_block, key_block, *far_keys)  4.77 us
    reshape x3, local copies, waits for them, and re-layouts, to_heads(): pieces = rows.reshape(tokens, parts, features // parts).transpose(1, 0, 2)  4.59 us
    pallas_call x1, Pallas kernels, shards(): return to_tokens(value(table, weights, totals, value_block, *far_values))  3.07 us
  transfers between devices with their start and end apart: 19, of which 6 were waited for; matrix products, arithmetic and copies ran while one was open for 6% of the time, Pallas kernels for 4%

profile of v2, /device:TPU:1, one launch (start us, length us, event | category | flops | bytes accessed | tf_op | source)
XLA Modules:
  0.0 128.2 jit_solution(8891136593060149982)
XLA Ops:
  0.0 1.9 %copy.30 = bf16[6,8,8,640]{3,2,0,1:T(8,128)(2,1)} copy(bf16[6,8,8,640]{3,2,1,0:T(8,128)(2,1)} %bitcast.47) | data formatting | bytes 983040 | tf_op jit(solution)/shard_map/reshape | solution.py:30
  1.9 10.3 %all-to-all-start.1 = ((bf16[8,48,640]{2,1,0:T(8,128)(2,1)}), bf16[8,48,640]{2,1,0:T(8,128)(2,1)S(1)}, u32[]{:S(2)}, u32[]{:S(2)}) async-start(bf16[8,48,640]{2,1,0:T(8,128)(2,1)} %bitcast.35), calls=%async_computation.1 | async-start | bytes 983040 | tf_op jit(solution)/shard_map/all_to_all | solution.py:31
  12.2 1.9 %copy.29 = bf16[6,8,8,640]{3,2,0,1:T(8,128)(2,1)} copy(bf16[6,8,8,640]{3,2,1,0:T(8,128)(2,1)} %bitcast.48) | data formatting | bytes 983040 | tf_op jit(solution)/shard_map/reshape | solution.py:30
  14.0 7.3 %all-to-all-done.1 = bf16[8,48,640]{2,1,0:T(8,128)(2,1)S(1)} async-done(((bf16[8,48,640]{2,1,0:T(8,128)(2,1)}), bf16[8,48,640]{2,1,0:T(8,128)(2,1)S(1)}, u32[]{:S(2)}, u32[]{:S(2)}) %all-to-all-start.1) | async-done | bytes 491552 | tf_op jit(solution)/shard_map/all_to_all | solution.py:31
  21.3 4.3 %all-to-all-start.2 = ((bf16[8,48,640]{2,1,0:T(8,128)(2,1)}), bf16[8,48,640]{2,1,0:T(8,128)(2,1)S(1)}, u32[]{:S(2)}, u32[]{:S(2)}) async-start(bf16[8,48,640]{2,1,0:T(8,128)(2,1)} %bitcast.33), calls=%async_computation.2 | async-start | bytes 983040 | tf_op jit(solution)/shard_map/all_to_all | solution.py:31
  25.6 1.9 %collective-permute-start.3 = (bf16[384,640]{1,0:T(8,128)(2,1)S(1)}, bf16[384,640]{1,0:T(8,128)(2,1)S(1)}, u32[]{:S(2)}, u32[]{:S(2)}) collective-permute-start(bf16[384,640]{1,0:T(8,128)(2,1)S(1)} %bitcast.38), channel_id=1, source_target_pairs={{0,64},{8,72},{16,80},{24,88},{32,96},{40,104},{48,112},{56,120},{... | collective-permute-start | bytes 1474568 | tf_op jit(solution)/shard_map/ppermute | solution.py:24
  27.5 6.2 %collective-permute-start = (bf16[384,640]{1,0:T(8,128)(2,1)S(1)}, bf16[384,640]{1,0:T(8,128)(2,1)S(1)}, u32[]{:S(2)}, u32[]{:S(2)}) collective-permute-start(bf16[384,640]{1,0:T(8,128)(2,1)S(1)} %bitcast.39), channel_id=1, source_target_pairs={{0,448},{8,456},{16,464},{24,472},{32,480},{40,488},{48,496},{56,5... | collective-permute-start | bytes 1474568 | tf_op jit(solution)/shard_map/ppermute | solution.py:24
  33.7 1.0 all-to-all-done.2
  34.7 1.9 %collective-permute-start.11 = (bf16[384,640]{1,0:T(8,128)(2,1)S(1)}, bf16[384,640]{1,0:T(8,128)(2,1)S(1)}, u32[]{:S(2)}, u32[]{:S(2)}) collective-permute-start(bf16[384,640]{1,0:T(8,128)(2,1)S(1)} %bitcast.42), channel_id=1, source_target_pairs={{0,64},{8,72},{16,80},{24,88},{32,96},{40,104},{48,112},{56,120},{... | collective-permute-start | bytes 1474568 | tf_op jit(solution)/shard_map/ppermute | solution.py:24
  36.6 6.2 %collective-permute-start.8 = (bf16[384,640]{1,0:T(8,128)(2,1)S(1)}, bf16[384,640]{1,0:T(8,128)(2,1)S(1)}, u32[]{:S(2)}, u32[]{:S(2)}) collective-permute-start(bf16[384,640]{1,0:T(8,128)(2,1)S(1)} %bitcast.43), channel_id=1, source_target_pairs={{0,448},{8,456},{16,464},{24,472},{32,480},{40,488},{48,496},{56,5... | collective-permute-start | bytes 1474568 | tf_op jit(solution)/shard_map/ppermute | solution.py:24
  42.9 0.8 copy.31
  43.7 4.5 %all-to-all-start = ((bf16[8,48,640]{2,1,0:T(8,128)(2,1)}), bf16[8,48,640]{2,1,0:T(8,128)(2,1)S(1)}, u32[]{:S(2)}, u32[]{:S(2)}) async-start(bf16[8,48,640]{2,1,0:T(8,128)(2,1)} %bitcast.37), calls=%async_computation | async-start | bytes 983040 | tf_op jit(solution)/shard_map/all_to_all | solution.py:31
  48.2 1.9 %collective-permute-start.4 = (bf16[384,640]{1,0:T(8,128)(2,1)S(1)}, bf16[384,640]{1,0:T(8,128)(2,1)}, u32[]{:S(2)}, u32[]{:S(2)}) collective-permute-start(bf16[384,640]{1,0:T(8,128)(2,1)S(1)} %collective-permute-done.3.rest_5_), channel_id=1, source_target_pairs={{0,64},{8,72},{16,80},{24,88},{32,96},{40,104},{48,112},{56,120},{... | collective-permute-start | bytes 1474568 | tf_op jit(solution)/shard_map/ppermute | solution.py:24
  50.2 4.6 %collective-permute-start.1 = (bf16[384,640]{1,0:T(8,128)(2,1)S(1)}, bf16[384,640]{1,0:T(8,128)(2,1)}, u32[]{:S(2)}, u32[]{:S(2)}) collective-permute-start(bf16[384,640]{1,0:T(8,128)(2,1)S(1)} %collective-permute-done.rest_0_), channel_id=1, source_target_pairs={{0,448},{8,456},{16,464},{24,472},{32,480},{40,488},{48,496},{56,5... | collective-permute-start | bytes 1474568 | tf_op jit(solution)/shard_map/ppermute | solution.py:24
  54.8 0.1 dynamic-slice_remainder_fusion
  54.9 0.1 copy.16
  55.0 0.1 rem.76
  55.1 1.9 %collective-permute-start.12 = (bf16[384,640]{1,0:T(8,128)(2,1)S(1)}, bf16[384,640]{1,0:T(8,128)(2,1)}, u32[]{:S(2)}, u32[]{:S(2)}) collective-permute-start(bf16[384,640]{1,0:T(8,128)(2,1)S(1)} %collective-permute-done.11.rest_5_), channel_id=1, source_target_pairs={{0,64},{8,72},{16,80},{24,88},{32,96},{40,104},{48,112},{56,120},{... | collective-permute-start | bytes 1474568 | tf_op jit(solution)/shard_map/ppermute | solution.py:24
  57.0 4.6 %collective-permute-start.9 = (bf16[384,640]{1,0:T(8,128)(2,1)S(1)}, bf16[384,640]{1,0:T(8,128)(2,1)}, u32[]{:S(2)}, u32[]{:S(2)}) collective-permute-start(bf16[384,640]{1,0:T(8,128)(2,1)S(1)} %collective-permute-done.8.rest_0_), channel_id=1, source_target_pairs={{0,448},{8,456},{16,464},{24,472},{32,480},{40,488},{48,496},{56,5... | collective-permute-start | bytes 1474568 | tf_op jit(solution)/shard_map/ppermute | solution.py:24
  61.6 2.5 %collective-permute-done.4.rest_4_ = bf16[384,640]{1,0:T(8,128)(2,1)} collective-permute-done((bf16[384,640]{1,0:T(8,128)(2,1)S(1)}, bf16[384,640]{1,0:T(8,128)(2,1)}, u32[]{:S(2)}, u32[]{:S(2)}) %collective-permute-start.4) | collective-permute-done | bytes 491552 | tf_op jit(solution)/shard_map/ppermute | solution.py:24
  64.2 1.9 %collective-permute-start.5 = (bf16[384,640]{1,0:T(8,128)(2,1)}, bf16[384,640]{1,0:T(8,128)(2,1)S(1)}, u32[]{:S(2)}, u32[]{:S(2)}) collective-permute-start(bf16[384,640]{1,0:T(8,128)(2,1)} %collective-permute-done.4.rest_4_), channel_id=1, source_target_pairs={{0,64},{8,72},{16,80},{24,88},{32,96},{40,104},{48,112},{56,120},{... | collective-permute-start | bytes 1474568 | tf_op jit(solution)/shard_map/ppermute | solution.py:24
  66.1 4.6 %collective-permute-start.2 = (bf16[384,640]{1,0:T(8,128)(2,1)}, bf16[384,640]{1,0:T(8,128)(2,1)S(1)}, u32[]{:S(2)}, u32[]{:S(2)}) collective-permute-start(bf16[384,640]{1,0:T(8,128)(2,1)} %collective-permute-done.1.rest_1_), channel_id=1, source_target_pairs={{0,448},{8,456},{16,464},{24,472},{32,480},{40,488},{48,496},{56,5... | collective-permute-start | bytes 1474568 | tf_op jit(solution)/shard_map/ppermute | solution.py:24
  70.7 0.2 and_reduce_fusion
  70.9 3.8 %collective-permute-done.12.rest_4_ = bf16[384,640]{1,0:T(8,128)(2,1)} collective-permute-done((bf16[384,640]{1,0:T(8,128)(2,1)S(1)}, bf16[384,640]{1,0:T(8,128)(2,1)}, u32[]{:S(2)}, u32[]{:S(2)}) %collective-permute-start.12) | collective-permute-done | bytes 491552 | tf_op jit(solution)/shard_map/ppermute | solution.py:24
  74.7 1.9 %collective-permute-start.13 = (bf16[384,640]{1,0:T(8,128)(2,1)}, bf16[384,640]{1,0:T(8,128)(2,1)S(1)}, u32[]{:S(2)}, u32[]{:S(2)}) collective-permute-start(bf16[384,640]{1,0:T(8,128)(2,1)} %collective-permute-done.12.rest_4_), channel_id=1, source_target_pairs={{0,64},{8,72},{16,80},{24,88},{32,96},{40,104},{48,112},{56,120},{... | collective-permute-start | bytes 1474568 | tf_op jit(solution)/shard_map/ppermute | solution.py:24
  76.6 4.6 %collective-permute-start.10 = (bf16[384,640]{1,0:T(8,128)(2,1)}, bf16[384,640]{1,0:T(8,128)(2,1)S(1)}, u32[]{:S(2)}, u32[]{:S(2)}) collective-permute-start(bf16[384,640]{1,0:T(8,128)(2,1)} %collective-permute-done.9.rest_1_), channel_id=1, source_target_pairs={{0,448},{8,456},{16,464},{24,472},{32,480},{40,488},{48,496},{56,5... | collective-permute-start | bytes 1474568 | tf_op jit(solution)/shard_map/ppermute | solution.py:24
  81.2 0.1 fusion.4
  81.3 0.1 copy.17
  81.4 0.1 copy.15
  81.5 0.1 div.22
  81.6 0.1 copy.14
  81.7 0.1 and.55
  81.8 3.3 %collective-permute-done.5.rest_3_ = bf16[384,640]{1,0:T(8,128)(2,1)S(1)} collective-permute-done((bf16[384,640]{1,0:T(8,128)(2,1)}, bf16[384,640]{1,0:T(8,128)(2,1)S(1)}, u32[]{:S(2)}, u32[]{:S(2)}) %collective-permute-start.5) | collective-permute-done | bytes 491552 | tf_op jit(solution)/shard_map/ppermute | solution.py:24
  85.1 0.8 slice.27
  85.9 1.9 %collective-permute-start.6 = (bf16[192,640]{1,0:T(8,128)(2,1)}, bf16[192,640]{1,0:T(8,128)(2,1)}, u32[]{:S(2)}, u32[]{:S(2)}) collective-permute-start(bf16[192,640]{1,0:T(8,128)(2,1)} %slice.27), channel_id=1, source_target_pairs={{0,64},{8,72},{16,80},{24,88},{32,96},{40,104},{48,112},{56,120},{... | collective-permute-start | bytes 737288 | tf_op jit(solution)/shard_map/ppermute | solution.py:24
  87.8 0.8 slice.28
  88.6 4.6 %collective-permute-start.7 = (bf16[192,640]{1,0:T(8,128)(2,1)}, bf16[192,640]{1,0:T(8,128)(2,1)}, u32[]{:S(2)}, u32[]{:S(2)}) collective-permute-start(bf16[192,640]{1,0:T(8,128)(2,1)} %slice.28), channel_id=1, source_target_pairs={{0,448},{8,456},{16,464},{24,472},{32,480},{40,488},{48,496},{56,5... | collective-permute-start | bytes 737288 | tf_op jit(solution)/shard_map/ppermute | solution.py:24
  93.2 0.1 fusion.3
  93.3 2.4 %collective-permute-done.13.rest_3_ = bf16[384,640]{1,0:T(8,128)(2,1)S(1)} collective-permute-done((bf16[384,640]{1,0:T(8,128)(2,1)}, bf16[384,640]{1,0:T(8,128)(2,1)S(1)}, u32[]{:S(2)}, u32[]{:S(2)}) %collective-permute-start.13) | collective-permute-done | bytes 491552 | tf_op jit(solution)/shard_map/ppermute | solution.py:24
  95.7 0.8 slice.29
  96.4 1.9 %collective-permute-start.14 = (bf16[192,640]{1,0:T(8,128)(2,1)}, bf16[192,640]{1,0:T(8,128)(2,1)}, u32[]{:S(2)}, u32[]{:S(2)}) collective-permute-start(bf16[192,640]{1,0:T(8,128)(2,1)} %slice.29), channel_id=1, source_target_pairs={{0,64},{8,72},{16,80},{24,88},{32,96},{40,104},{48,112},{56,120},{... | collective-permute-start | bytes 737288 | tf_op jit(solution)/shard_map/ppermute | solution.py:24
  98.4 0.8 slice.30
  99.1 4.6 %collective-permute-start.15 = (bf16[192,640]{1,0:T(8,128)(2,1)}, bf16[192,640]{1,0:T(8,128)(2,1)}, u32[]{:S(2)}, u32[]{:S(2)}) collective-permute-start(bf16[192,640]{1,0:T(8,128)(2,1)} %slice.30), channel_id=1, source_target_pairs={{0,448},{8,456},{16,464},{24,472},{32,480},{40,488},{48,496},{56,5... | collective-permute-start | bytes 737288 | tf_op jit(solution)/shard_map/ppermute | solution.py:24
  103.7 0.1 fusion.1
  103.9 4.8 %scores.1 = (bf16[15,128,768]{2,1,0:T(8,128)(2,1)S(1)}, f32[3,128,128]{2,1,0:T(8,128)S(1)}) custom-call(s32[27]{0:T(128)S(1)} %pad_add_fusion.table, bf16[384,640]{1,0:T(8,128)(2,1)S(1)} %bitcast.41, bf16[384,640]{1,0:T(8,128)(2,1)S(1)} %bitcast.40, bf16[384,640]{1,0:T(8,128)(2,1)} %copy-done.6, bf16[384,640]{1,0:T(8,128)(2,1)} %collective-permute-done.1.rest_1_, ...), custom_call_target="tpu_custom_call" | custom-call | flops 377487360 | bytes 6291456 | tf_op jit(solution)/shard_map/scores/pallas_call | solution.py:228
  108.7 3.1 %weighted_values.1 = bf16[384,640]{1,0:T(8,128)(2,1)S(1)} custom-call(s32[27]{0:T(128)S(1)} %pad_add_fusion.table, bf16[15,128,768]{2,1,0:T(8,128)(2,1)S(1)} %get-tuple-element.7.w_ref, f32[3,128,128]{2,1,0:T(8,128)S(1)} %get-tuple-element.8.total_ref, bf16[384,640]{1,0:T(8,128)(2,1)S(1)} %bitcast.44, bf16[384,640]{1,0:T(8,128)(2,1)} %copy-done.8, ...), custom_call_target="tpu_custom_call" | custom-call | flops 377487360 | bytes 6291456 | tf_op jit(solution)/shard_map/weighted_values/pallas_call | solution.py:229
  111.8 15.6 %all_to_all.20 = bf16[8,48,640]{2,1,0:T(8,128)(2,1)S(1)} all-to-all(bf16[8,48,640]{2,1,0:T(8,128)(2,1)S(1)} %bitcast.45), channel_id=1, replica_groups=mesh['seq'=64,'head'=8] {'head'}, dimensions={0} | all-to-all | bytes 983040 | tf_op jit(solution)/shard_map/all_to_all | solution.py:39
  127.4 0.8 copy.25
  (42 shorter events, 0.2 us)
Async XLA Ops:
  0.0 42.8 %copy-start.4 = (bf16[48,5120]{1,0:T(8,128)(2,1)S(1)}, bf16[48,5120]{1,0:T(8,128)(2,1)}, u32[]{:S(2)}) copy-start(bf16[48,5120]{1,0:T(8,128)(2,1)} %param.5) | copy-start | bytes 1474564
  0.0 48.2 %copy-start.10 = (s32[24,2]{0,1:T(2,128)S(1)}, s32[24,2]{0,1:T(2,128)}, u32[]{:S(2)}) copy-start(s32[24,2]{0,1:T(2,128)} %param.9) | copy-start | bytes 580
  0.0 54.8 %copy-start.9 = (s32[192,3]{0,1:T(4,128)S(1)}, s32[192,3]{0,1:T(4,128)}, u32[]{:S(2)}) copy-start(s32[192,3]{0,1:T(4,128)} %param.8) | copy-start | bytes 6916
  1.9 19.4 %all-to-all-start.1 = ((bf16[8,48,640]{2,1,0:T(8,128)(2,1)}), bf16[8,48,640]{2,1,0:T(8,128)(2,1)S(1)}, u32[]{:S(2)}, u32[]{:S(2)}) async-start(bf16[8,48,640]{2,1,0:T(8,128)(2,1)} %bitcast.35), calls=%async_computation.1 | async-start | bytes 983040 | tf_op jit(solution)/shard_map/all_to_all | solution.py:31
  21.3 13.4 %all-to-all-start.2 = ((bf16[8,48,640]{2,1,0:T(8,128)(2,1)}), bf16[8,48,640]{2,1,0:T(8,128)(2,1)S(1)}, u32[]{:S(2)}, u32[]{:S(2)}) async-start(bf16[8,48,640]{2,1,0:T(8,128)(2,1)} %bitcast.33), calls=%async_computation.2 | async-start | bytes 983040 | tf_op jit(solution)/shard_map/all_to_all | solution.py:31
  25.6 22.6 %collective-permute-start.3 = (bf16[384,640]{1,0:T(8,128)(2,1)S(1)}, bf16[384,640]{1,0:T(8,128)(2,1)S(1)}, u32[]{:S(2)}, u32[]{:S(2)}) collective-permute-start(bf16[384,640]{1,0:T(8,128)(2,1)S(1)} %bitcast.38), channel_id=1, source_target_pairs={{0,64},{8,72},{16,80},{24,88},{32,96},{40,104},{48,112},{56,120},{... | collective-permute-start | bytes 1474568 | tf_op jit(solution)/shard_map/ppermute | solution.py:24
  27.5 22.7 %collective-permute-start = (bf16[384,640]{1,0:T(8,128)(2,1)S(1)}, bf16[384,640]{1,0:T(8,128)(2,1)S(1)}, u32[]{:S(2)}, u32[]{:S(2)}) collective-permute-start(bf16[384,640]{1,0:T(8,128)(2,1)S(1)} %bitcast.39), channel_id=1, source_target_pairs={{0,448},{8,456},{16,464},{24,472},{32,480},{40,488},{48,496},{56,5... | collective-permute-start | bytes 1474568 | tf_op jit(solution)/shard_map/ppermute | solution.py:24
  34.7 20.3 %collective-permute-start.11 = (bf16[384,640]{1,0:T(8,128)(2,1)S(1)}, bf16[384,640]{1,0:T(8,128)(2,1)S(1)}, u32[]{:S(2)}, u32[]{:S(2)}) collective-permute-start(bf16[384,640]{1,0:T(8,128)(2,1)S(1)} %bitcast.42), channel_id=1, source_target_pairs={{0,64},{8,72},{16,80},{24,88},{32,96},{40,104},{48,112},{56,120},{... | collective-permute-start | bytes 1474568 | tf_op jit(solution)/shard_map/ppermute | solution.py:24
  36.6 20.3 %collective-permute-start.8 = (bf16[384,640]{1,0:T(8,128)(2,1)S(1)}, bf16[384,640]{1,0:T(8,128)(2,1)S(1)}, u32[]{:S(2)}, u32[]{:S(2)}) collective-permute-start(bf16[384,640]{1,0:T(8,128)(2,1)S(1)} %bitcast.43), channel_id=1, source_target_pairs={{0,448},{8,456},{16,464},{24,472},{32,480},{40,488},{48,496},{56,5... | collective-permute-start | bytes 1474568 | tf_op jit(solution)/shard_map/ppermute | solution.py:24
  43.7 60.2 %all-to-all-start = ((bf16[8,48,640]{2,1,0:T(8,128)(2,1)}), bf16[8,48,640]{2,1,0:T(8,128)(2,1)S(1)}, u32[]{:S(2)}, u32[]{:S(2)}) async-start(bf16[8,48,640]{2,1,0:T(8,128)(2,1)} %bitcast.37), calls=%async_computation | async-start | bytes 983040 | tf_op jit(solution)/shard_map/all_to_all | solution.py:31
  48.2 13.4 %copy-start.5 = (bf16[384,640]{1,0:T(8,128)(2,1)}, bf16[384,640]{1,0:T(8,128)(2,1)S(1)}, u32[]{:S(2)}) copy-start(bf16[384,640]{1,0:T(8,128)(2,1)S(1)} %collective-permute-done.3.rest_5_) | copy-start | bytes 1474564
  48.2 15.9 %collective-permute-start.4 = (bf16[384,640]{1,0:T(8,128)(2,1)S(1)}, bf16[384,640]{1,0:T(8,128)(2,1)}, u32[]{:S(2)}, u32[]{:S(2)}) collective-permute-start(bf16[384,640]{1,0:T(8,128)(2,1)S(1)} %collective-permute-done.3.rest_5_), channel_id=1, source_target_pairs={{0,64},{8,72},{16,80},{24,88},{32,96},{40,104},{48,112},{56,120},{... | collective-permute-start | bytes 1474568 | tf_op jit(solution)/shard_map/ppermute | solution.py:24
  50.2 15.9 %copy-start.6 = (bf16[384,640]{1,0:T(8,128)(2,1)}, bf16[384,640]{1,0:T(8,128)(2,1)S(1)}, u32[]{:S(2)}) copy-start(bf16[384,640]{1,0:T(8,128)(2,1)S(1)} %collective-permute-done.rest_0_) | copy-start | bytes 1474564
  50.2 15.9 %collective-permute-start.1 = (bf16[384,640]{1,0:T(8,128)(2,1)S(1)}, bf16[384,640]{1,0:T(8,128)(2,1)}, u32[]{:S(2)}, u32[]{:S(2)}) collective-permute-start(bf16[384,640]{1,0:T(8,128)(2,1)S(1)} %collective-permute-done.rest_0_), channel_id=1, source_target_pairs={{0,448},{8,456},{16,464},{24,472},{32,480},{40,488},{48,496},{56,5... | collective-permute-start | bytes 1474568 | tf_op jit(solution)/shard_map/ppermute | solution.py:24
  55.1 15.8 %copy-start.7 = (bf16[384,640]{1,0:T(8,128)(2,1)}, bf16[384,640]{1,0:T(8,128)(2,1)S(1)}, u32[]{:S(2)}) copy-start(bf16[384,640]{1,0:T(8,128)(2,1)S(1)} %collective-permute-done.11.rest_5_) | copy-start | bytes 1474564
  55.1 19.6 %collective-permute-start.12 = (bf16[384,640]{1,0:T(8,128)(2,1)S(1)}, bf16[384,640]{1,0:T(8,128)(2,1)}, u32[]{:S(2)}, u32[]{:S(2)}) collective-permute-start(bf16[384,640]{1,0:T(8,128)(2,1)S(1)} %collective-permute-done.11.rest_5_), channel_id=1, source_target_pairs={{0,64},{8,72},{16,80},{24,88},{32,96},{40,104},{48,112},{56,120},{... | collective-permute-start | bytes 1474568 | tf_op jit(solution)/shard_map/ppermute | solution.py:24
  57.0 19.6 %copy-start.8 = (bf16[384,640]{1,0:T(8,128)(2,1)}, bf16[384,640]{1,0:T(8,128)(2,1)S(1)}, u32[]{:S(2)}) copy-start(bf16[384,640]{1,0:T(8,128)(2,1)S(1)} %collective-permute-done.8.rest_0_) | copy-start | bytes 1474564
  57.0 19.6 %collective-permute-start.9 = (bf16[384,640]{1,0:T(8,128)(2,1)S(1)}, bf16[384,640]{1,0:T(8,128)(2,1)}, u32[]{:S(2)}, u32[]{:S(2)}) collective-permute-start(bf16[384,640]{1,0:T(8,128)(2,1)S(1)} %collective-permute-done.8.rest_0_), channel_id=1, source_target_pairs={{0,448},{8,456},{16,464},{24,472},{32,480},{40,488},{48,496},{56,5... | collective-permute-start | bytes 1474568 | tf_op jit(solution)/shard_map/ppermute | solution.py:24
  64.2 21.0 %collective-permute-start.5 = (bf16[384,640]{1,0:T(8,128)(2,1)}, bf16[384,640]{1,0:T(8,128)(2,1)S(1)}, u32[]{:S(2)}, u32[]{:S(2)}) collective-permute-start(bf16[384,640]{1,0:T(8,128)(2,1)} %collective-permute-done.4.rest_4_), channel_id=1, source_target_pairs={{0,64},{8,72},{16,80},{24,88},{32,96},{40,104},{48,112},{56,120},{... | collective-permute-start | bytes 1474568 | tf_op jit(solution)/shard_map/ppermute | solution.py:24
  66.1 21.7 %collective-permute-start.2 = (bf16[384,640]{1,0:T(8,128)(2,1)}, bf16[384,640]{1,0:T(8,128)(2,1)S(1)}, u32[]{:S(2)}, u32[]{:S(2)}) collective-permute-start(bf16[384,640]{1,0:T(8,128)(2,1)} %collective-permute-done.1.rest_1_), channel_id=1, source_target_pairs={{0,448},{8,456},{16,464},{24,472},{32,480},{40,488},{48,496},{56,5... | collective-permute-start | bytes 1474568 | tf_op jit(solution)/shard_map/ppermute | solution.py:24
  74.7 21.0 %collective-permute-start.13 = (bf16[384,640]{1,0:T(8,128)(2,1)}, bf16[384,640]{1,0:T(8,128)(2,1)S(1)}, u32[]{:S(2)}, u32[]{:S(2)}) collective-permute-start(bf16[384,640]{1,0:T(8,128)(2,1)} %collective-permute-done.12.rest_4_), channel_id=1, source_target_pairs={{0,64},{8,72},{16,80},{24,88},{32,96},{40,104},{48,112},{56,120},{... | collective-permute-start | bytes 1474568 | tf_op jit(solution)/shard_map/ppermute | solution.py:24
  76.6 21.7 %collective-permute-start.10 = (bf16[384,640]{1,0:T(8,128)(2,1)}, bf16[384,640]{1,0:T(8,128)(2,1)S(1)}, u32[]{:S(2)}, u32[]{:S(2)}) collective-permute-start(bf16[384,640]{1,0:T(8,128)(2,1)} %collective-permute-done.9.rest_1_), channel_id=1, source_target_pairs={{0,448},{8,456},{16,464},{24,472},{32,480},{40,488},{48,496},{56,5... | collective-permute-start | bytes 1474568 | tf_op jit(solution)/shard_map/ppermute | solution.py:24
  85.1 18.8 %copy-start = (bf16[384,640]{1,0:T(8,128)(2,1)}, bf16[384,640]{1,0:T(8,128)(2,1)S(1)}, u32[]{:S(2)}) copy-start(bf16[384,640]{1,0:T(8,128)(2,1)S(1)} %collective-permute-done.5.rest_3_) | copy-start | bytes 1474564
  85.9 18.0 %collective-permute-start.6 = (bf16[192,640]{1,0:T(8,128)(2,1)}, bf16[192,640]{1,0:T(8,128)(2,1)}, u32[]{:S(2)}, u32[]{:S(2)}) collective-permute-start(bf16[192,640]{1,0:T(8,128)(2,1)} %slice.27), channel_id=1, source_target_pairs={{0,64},{8,72},{16,80},{24,88},{32,96},{40,104},{48,112},{56,120},{... | collective-permute-start | bytes 737288 | tf_op jit(solution)/shard_map/ppermute | solution.py:24
  87.8 16.1 %copy-start.1 = (bf16[384,640]{1,0:T(8,128)(2,1)}, bf16[384,640]{1,0:T(8,128)(2,1)S(1)}, u32[]{:S(2)}) copy-start(bf16[384,640]{1,0:T(8,128)(2,1)S(1)} %collective-permute-done.2.rest_2_) | copy-start | bytes 1474564
  88.6 15.3 %collective-permute-start.7 = (bf16[192,640]{1,0:T(8,128)(2,1)}, bf16[192,640]{1,0:T(8,128)(2,1)}, u32[]{:S(2)}, u32[]{:S(2)}) collective-permute-start(bf16[192,640]{1,0:T(8,128)(2,1)} %slice.28), channel_id=1, source_target_pairs={{0,448},{8,456},{16,464},{24,472},{32,480},{40,488},{48,496},{56,5... | collective-permute-start | bytes 737288 | tf_op jit(solution)/shard_map/ppermute | solution.py:24
  95.7 13.0 %copy-start.2 = (bf16[384,640]{1,0:T(8,128)(2,1)}, bf16[384,640]{1,0:T(8,128)(2,1)S(1)}, u32[]{:S(2)}) copy-start(bf16[384,640]{1,0:T(8,128)(2,1)S(1)} %collective-permute-done.13.rest_3_) | copy-start | bytes 1474564
  96.4 12.3 %collective-permute-start.14 = (bf16[192,640]{1,0:T(8,128)(2,1)}, bf16[192,640]{1,0:T(8,128)(2,1)}, u32[]{:S(2)}, u32[]{:S(2)}) collective-permute-start(bf16[192,640]{1,0:T(8,128)(2,1)} %slice.29), channel_id=1, source_target_pairs={{0,64},{8,72},{16,80},{24,88},{32,96},{40,104},{48,112},{56,120},{... | collective-permute-start | bytes 737288 | tf_op jit(solution)/shard_map/ppermute | solution.py:24
  98.3 10.4 %copy-start.3 = (bf16[384,640]{1,0:T(8,128)(2,1)}, bf16[384,640]{1,0:T(8,128)(2,1)S(1)}, u32[]{:S(2)}) copy-start(bf16[384,640]{1,0:T(8,128)(2,1)S(1)} %collective-permute-done.10.rest_2_) | copy-start | bytes 1474564
  99.1 9.6 %collective-permute-start.15 = (bf16[192,640]{1,0:T(8,128)(2,1)}, bf16[192,640]{1,0:T(8,128)(2,1)}, u32[]{:S(2)}, u32[]{:S(2)}) collective-permute-start(bf16[192,640]{1,0:T(8,128)(2,1)} %slice.30), channel_id=1, source_target_pairs={{0,448},{8,456},{16,464},{24,472},{32,480},{40,488},{48,496},{56,5... | collective-permute-start | bytes 737288 | tf_op jit(solution)/shard_map/ppermute | solution.py:24

commit v3 on v2

--- a/solution.py
+++ b/solution.py
@@ -14,7 +14,6 @@
 SHOTS = 8
 PER_BLOCK = 3
 FAR = PER_BLOCK * ROUTED
-HALF = GROUP // 2
 
 
 def hop(value, axis, shots):
@@ -85,18 +84,17 @@
             def _(place=place):
                 copy(far[place], pl.multiple_of(group * GROUP, GROUP), slot, 0, GROUP)
 
-        @pl.when((away == 4) & (group == 0))
-        def _():
-            copy(far[6], 0, slot, 0, GROUP)
-
-        @pl.when((away == 4) & (group == 1))
-        def _():
-            copy(far[6], GROUP, slot, 0, HALF)
-            copy(far[7], 0, slot, HALF, HALF)
-
-        @pl.when((away == 4) & (group == 2))
-        def _():
-            copy(far[7], HALF, slot, 0, GROUP)
+        split = far[6].shape[0]
+        for g in range(PER_BLOCK):
+
+            @pl.when((away == 4) & (group == g))
+            def _(g=g):
+                first = g * GROUP
+                cut = min(max(split - first, 0), GROUP)
+                if cut > 0:
+                    copy(far[6], first, slot, 0, cut)
+                if cut < GROUP:
+                    copy(far[7], first + cut - split, slot, cut, GROUP - cut)
 
         return carry
 
@@ -109,7 +107,7 @@
 
 
 def score_kernel(table, q_ref, k_ref, *rest):
-    far, (w_ref, total_ref, buffer, sems) = rest[:8], rest[8:]
+    far, (near_ref, far_ref, total_ref, buffer, sems) = rest[:8], rest[8:]
     fetch(table, far, buffer, sems)
     heads = q_ref.shape[1] // HD
     tokens = k_ref.shape[0]
@@ -139,31 +137,32 @@
             weights = jnp.exp(scores - jnp.max(scores, axis=1, keepdims=True))
             total = jnp.sum(weights, axis=1, keepdims=True)
             totals = jnp.where(lanes == h, total, totals)
-            w_ref[c * heads + h] = weights.astype(jnp.bfloat16)
+            weights = weights.astype(jnp.bfloat16)
+            near_ref[h, rows, :] = weights[:, :tokens]
+            far_ref[c * heads + h] = weights[:, tokens:]
         total_ref[c] = totals
 
 
-def value_kernel(table, w_ref, total_ref, v_ref, *rest):
-    far, (o_ref, buffer, sems) = rest[:8], rest[8:]
+def value_kernel(table, near_ref, far_ref, total_ref, v_ref, *rest):
+    far, (o_ref, buffer, partial, sems) = rest[:8], rest[8:]
     fetch(table, far, buffer, sems)
     tokens, features = v_ref.shape
     heads = features // HD
+    for h in range(heads):
+        columns = slice(h * HD, (h + 1) * HD)
+        partial[:, columns] = jnp.dot(
+            near_ref[h], v_ref[:, columns], preferred_element_type=jnp.float32
+        )
     for c in range(PER_BLOCK):
         arrived(buffer, sems, c)
         rows = slice(c * GROUP, (c + 1) * GROUP)
+        slots = slice(c * ROUTED, (c + 1) * ROUTED)
         for h in range(heads):
             columns = slice(h * HD, (h + 1) * HD)
-            weights = w_ref[c * heads + h]
-            result = jnp.dot(
-                weights[:, :tokens], v_ref[:, columns], preferred_element_type=jnp.float32
+            far_values = buffer[slots, :, columns].reshape(ROUTED * GROUP, HD)
+            result = partial[rows, columns] + jnp.dot(
+                far_ref[c * heads + h], far_values, preferred_element_type=jnp.float32
             )
-            for j in range(ROUTED):
-                at = tokens + j * GROUP
-                result += jnp.dot(
-                    weights[:, at : at + GROUP],
-                    buffer[c * ROUTED + j, :, columns],
-                    preferred_element_type=jnp.float32,
-                )
             o_ref[rows, columns] = (result / total_ref[c][:, h : h + 1]).astype(o_ref.dtype)
 
 
@@ -180,11 +179,12 @@
     score = pl.pallas_call(
         score_kernel,
         out_shape=(
-            jax.ShapeDtypeStruct((PER_BLOCK * heads, GROUP, keys), jnp.bfloat16),
+            jax.ShapeDtypeStruct((heads, PER_BLOCK * GROUP, PER_BLOCK * GROUP), jnp.bfloat16),
+            jax.ShapeDtypeStruct((PER_BLOCK * heads, GROUP, ROUTED * GROUP), jnp.bfloat16),
             jax.ShapeDtypeStruct((PER_BLOCK, GROUP, HD), jnp.float32),
         ),
         in_specs=[SMEM, VMEM, VMEM] + [ANY] * 8,
-        out_specs=(VMEM, VMEM),
+        out_specs=(VMEM, VMEM, VMEM),
         scratch_shapes=scratch,
         compiler_params=pltpu.CompilerParams(vmem_limit_bytes=24 << 20),
         cost_estimate=pl.CostEstimate(
@@ -195,9 +195,13 @@
     value = pl.pallas_call(
         value_kernel,
         out_shape=jax.ShapeDtypeStruct((PER_BLOCK * GROUP, features), jnp.bfloat16),
-        in_specs=[SMEM, VMEM, VMEM, VMEM] + [ANY] * 8,
+        in_specs=[SMEM, VMEM, VMEM, VMEM, VMEM] + [ANY] * 8,
         out_specs=VMEM,
-        scratch_shapes=scratch,
+        scratch_shapes=[
+            scratch[0],
+            pltpu.VMEM((PER_BLOCK * GROUP, features), jnp.float32),
+            scratch[1],
+        ],
         compiler_params=pltpu.CompilerParams(vmem_limit_bytes=24 << 20),
         cost_estimate=pl.CostEstimate(flops=flops, bytes_accessed=6 << 20, transcendentals=0),
         name="weighted_values",
@@ -220,13 +224,14 @@
     v_up3, v_down3 = up(v_up2), down(v_down2)
     middle = key_block.shape[0] // 2
     k_upper, k_lower = up(k_up3[:middle]), down(k_down3[middle:])
-    v_upper, v_lower = up(v_up3[:middle]), down(v_down3[middle:])
+    more = middle + GROUP // 4
+    v_upper, v_lower = up(v_up3[:more]), down(v_down3[more:])
     score, value = kernels(key_block.shape[1])
     far_keys = (k_down1, k_down2, k_down3, k_up3, k_up2, k_up1, k_upper, k_lower)
     far_values = (v_down1, v_down2, v_down3, v_up3, v_up2, v_up1, v_upper, v_lower)
     far_keys, far_values = in_hbm(far_keys), in_hbm(far_values)
-    weights, totals = score(table, query_block, key_block, *far_keys)
-    return to_tokens(value(table, weights, totals, value_block, *far_values))
+    near, routed, totals = score(table, query_block, key_block, *far_keys)
+    return to_tokens(value(table, near, routed, totals, value_block, *far_values))
 
 
 def solution(mesh):

time: 129 us -> 129 us (level)
  transfers between devices with their start and end apart: 19 -> 19, of which waited for: 6 -> 6; matrix products, arithmetic and copies ran while one was open for 6% -> 5% of each run, Pallas kernels for 4% -> 4%
where the time goes in v3:
time: 129 us; the launch traced here: 128 us
  starting transfers between devices  74.4 us (58%)
  waiting for transfers between devices  21.5 us (17%)
  blocking collectives  15.6 us (12%)
  local copies, waits for them, and re-layouts  8.14 us (6%)
  Pallas kernels  7.39 us (6%)
    ppermute x16, starting transfers between devices, hop(): return lax.ppermute(value, axis, pairs)  55.1 us
    all_to_all x3, starting transfers between devices, to_heads(): lax.all_to_all(pieces, 'head', split_axis=0, concat_axis=0, tiled=True)  19.3 us
    all_to_all x1, blocking collectives, to_tokens(): lax.all_to_all(pieces, 'head', split_axis=0, concat_axis=0, tiled=True)  15.6 us
    ppermute x16, waiting for transfers between devices, hop(): return lax.ppermute(value, axis, pairs)  12.2 us
    all_to_all x3, waiting for transfers between devices, to_heads(): lax.all_to_all(pieces, 'head', split_axis=0, concat_axis=0, tiled=True)  9.35 us
    pallas_call x1, Pallas kernels, shards(): near, routed, totals = score(table, query_block, key_block, *far_keys)  4.79 us
    reshape x3, local copies, waits for them, and re-layouts, to_heads(): pieces = rows.reshape(tokens, parts, features // parts).transpose(1, 0, 2)  3.56 us
    pallas_call x1, Pallas kernels, shards(): value(table, near, routed, totals, value_block, *far_values)  2.6 us
  transfers between devices with their start and end apart: 19, of which 6 were waited for; matrix products, arithmetic and copies ran while one was open for 5% of the time, Pallas kernels for 4%

profile of v3, /device:TPU:1, one launch (start us, length us, event | category | flops | bytes accessed | tf_op | source)
XLA Modules:
  0.0 128.1 jit_solution(4512259174424538141)
XLA Ops:
  0.0 1.9 %copy.30 = bf16[6,8,8,640]{3,2,0,1:T(8,128)(2,1)} copy(bf16[6,8,8,640]{3,2,1,0:T(8,128)(2,1)} %bitcast.47) | data formatting | bytes 983040 | tf_op jit(solution)/shard_map/reshape | solution.py:29
  1.9 10.4 %all-to-all-start.1 = ((bf16[8,48,640]{2,1,0:T(8,128)(2,1)}), bf16[8,48,640]{2,1,0:T(8,128)(2,1)S(1)}, u32[]{:S(2)}, u32[]{:S(2)}) async-start(bf16[8,48,640]{2,1,0:T(8,128)(2,1)} %bitcast.35), calls=%async_computation.1 | async-start | bytes 983040 | tf_op jit(solution)/shard_map/all_to_all | solution.py:30
  12.3 0.8 copy.29
  13.1 8.3 %all-to-all-done.1 = bf16[8,48,640]{2,1,0:T(8,128)(2,1)S(1)} async-done(((bf16[8,48,640]{2,1,0:T(8,128)(2,1)}), bf16[8,48,640]{2,1,0:T(8,128)(2,1)S(1)}, u32[]{:S(2)}, u32[]{:S(2)}) %all-to-all-start.1) | async-done | bytes 491552 | tf_op jit(solution)/shard_map/all_to_all | solution.py:30
  21.5 4.4 %all-to-all-start.2 = ((bf16[8,48,640]{2,1,0:T(8,128)(2,1)}), bf16[8,48,640]{2,1,0:T(8,128)(2,1)S(1)}, u32[]{:S(2)}, u32[]{:S(2)}) async-start(bf16[8,48,640]{2,1,0:T(8,128)(2,1)} %bitcast.33), calls=%async_computation.2 | async-start | bytes 983040 | tf_op jit(solution)/shard_map/all_to_all | solution.py:30
  25.8 1.9 %collective-permute-start.3 = (bf16[384,640]{1,0:T(8,128)(2,1)S(1)}, bf16[384,640]{1,0:T(8,128)(2,1)S(1)}, u32[]{:S(2)}, u32[]{:S(2)}) collective-permute-start(bf16[384,640]{1,0:T(8,128)(2,1)S(1)} %bitcast.38), channel_id=1, source_target_pairs={{0,64},{8,72},{16,80},{24,88},{32,96},{40,104},{48,112},{56,120},{... | collective-permute-start | bytes 1474568 | tf_op jit(solution)/shard_map/ppermute | solution.py:23
  27.8 6.2 %collective-permute-start = (bf16[384,640]{1,0:T(8,128)(2,1)S(1)}, bf16[384,640]{1,0:T(8,128)(2,1)S(1)}, u32[]{:S(2)}, u32[]{:S(2)}) collective-permute-start(bf16[384,640]{1,0:T(8,128)(2,1)S(1)} %bitcast.39), channel_id=1, source_target_pairs={{0,448},{8,456},{16,464},{24,472},{32,480},{40,488},{48,496},{56,5... | collective-permute-start | bytes 1474568 | tf_op jit(solution)/shard_map/ppermute | solution.py:23
  34.0 1.0 all-to-all-done.2
  35.0 1.9 %collective-permute-start.11 = (bf16[384,640]{1,0:T(8,128)(2,1)S(1)}, bf16[384,640]{1,0:T(8,128)(2,1)S(1)}, u32[]{:S(2)}, u32[]{:S(2)}) collective-permute-start(bf16[384,640]{1,0:T(8,128)(2,1)S(1)} %bitcast.42), channel_id=1, source_target_pairs={{0,64},{8,72},{16,80},{24,88},{32,96},{40,104},{48,112},{56,120},{... | collective-permute-start | bytes 1474568 | tf_op jit(solution)/shard_map/ppermute | solution.py:23
  36.9 6.2 %collective-permute-start.8 = (bf16[384,640]{1,0:T(8,128)(2,1)S(1)}, bf16[384,640]{1,0:T(8,128)(2,1)}, u32[]{:S(2)}, u32[]{:S(2)}) collective-permute-start(bf16[384,640]{1,0:T(8,128)(2,1)S(1)} %bitcast.43), channel_id=1, source_target_pairs={{0,448},{8,456},{16,464},{24,472},{32,480},{40,488},{48,496},{56,5... | collective-permute-start | bytes 1474568 | tf_op jit(solution)/shard_map/ppermute | solution.py:23
  43.1 0.8 copy.31
  43.9 4.5 %all-to-all-start = ((bf16[8,48,640]{2,1,0:T(8,128)(2,1)}), bf16[8,48,640]{2,1,0:T(8,128)(2,1)S(1)}, u32[]{:S(2)}, u32[]{:S(2)}) async-start(bf16[8,48,640]{2,1,0:T(8,128)(2,1)} %bitcast.37), calls=%async_computation | async-start | bytes 983040 | tf_op jit(solution)/shard_map/all_to_all | solution.py:30
  48.5 1.9 %collective-permute-start.4 = (bf16[384,640]{1,0:T(8,128)(2,1)S(1)}, bf16[384,640]{1,0:T(8,128)(2,1)}, u32[]{:S(2)}, u32[]{:S(2)}) collective-permute-start(bf16[384,640]{1,0:T(8,128)(2,1)S(1)} %collective-permute-done.3.rest_5_), channel_id=1, source_target_pairs={{0,64},{8,72},{16,80},{24,88},{32,96},{40,104},{48,112},{56,120},{... | collective-permute-start | bytes 1474568 | tf_op jit(solution)/shard_map/ppermute | solution.py:23
  50.5 4.6 %collective-permute-start.1 = (bf16[384,640]{1,0:T(8,128)(2,1)S(1)}, bf16[384,640]{1,0:T(8,128)(2,1)}, u32[]{:S(2)}, u32[]{:S(2)}) collective-permute-start(bf16[384,640]{1,0:T(8,128)(2,1)S(1)} %collective-permute-done.rest_0_), channel_id=1, source_target_pairs={{0,448},{8,456},{16,464},{24,472},{32,480},{40,488},{48,496},{56,5... | collective-permute-start | bytes 1474568 | tf_op jit(solution)/shard_map/ppermute | solution.py:23
  55.1 1.9 %collective-permute-start.12 = (bf16[384,640]{1,0:T(8,128)(2,1)S(1)}, bf16[384,640]{1,0:T(8,128)(2,1)}, u32[]{:S(2)}, u32[]{:S(2)}) collective-permute-start(bf16[384,640]{1,0:T(8,128)(2,1)S(1)} %collective-permute-done.11.rest_5_), channel_id=1, source_target_pairs={{0,64},{8,72},{16,80},{24,88},{32,96},{40,104},{48,112},{56,120},{... | collective-permute-start | bytes 1474568 | tf_op jit(solution)/shard_map/ppermute | solution.py:23
  57.0 0.1 dynamic-slice_remainder_fusion
  57.1 0.1 copy.16
  57.2 0.1 rem.76
  57.3 4.6 %collective-permute-start.9 = (bf16[384,640]{1,0:T(8,128)(2,1)}, bf16[384,640]{1,0:T(8,128)(2,1)}, u32[]{:S(2)}, u32[]{:S(2)}) collective-permute-start(bf16[384,640]{1,0:T(8,128)(2,1)} %collective-permute-done.8.rest_0_), channel_id=1, source_target_pairs={{0,448},{8,456},{16,464},{24,472},{32,480},{40,488},{48,496},{56,5... | collective-permute-start | bytes 1474568 | tf_op jit(solution)/shard_map/ppermute | solution.py:23
  61.9 2.5 %collective-permute-done.4.rest_4_ = bf16[384,640]{1,0:T(8,128)(2,1)} collective-permute-done((bf16[384,640]{1,0:T(8,128)(2,1)S(1)}, bf16[384,640]{1,0:T(8,128)(2,1)}, u32[]{:S(2)}, u32[]{:S(2)}) %collective-permute-start.4) | collective-permute-done | bytes 491552 | tf_op jit(solution)/shard_map/ppermute | solution.py:23
  64.4 1.9 %collective-permute-start.5 = (bf16[384,640]{1,0:T(8,128)(2,1)}, bf16[384,640]{1,0:T(8,128)(2,1)S(1)}, u32[]{:S(2)}, u32[]{:S(2)}) collective-permute-start(bf16[384,640]{1,0:T(8,128)(2,1)} %collective-permute-done.4.rest_4_), channel_id=1, source_target_pairs={{0,64},{8,72},{16,80},{24,88},{32,96},{40,104},{48,112},{56,120},{... | collective-permute-start | bytes 1474568 | tf_op jit(solution)/shard_map/ppermute | solution.py:23
  66.4 4.6 %collective-permute-start.2 = (bf16[384,640]{1,0:T(8,128)(2,1)}, bf16[384,640]{1,0:T(8,128)(2,1)S(1)}, u32[]{:S(2)}, u32[]{:S(2)}) collective-permute-start(bf16[384,640]{1,0:T(8,128)(2,1)} %collective-permute-done.1.rest_1_), channel_id=1, source_target_pairs={{0,448},{8,456},{16,464},{24,472},{32,480},{40,488},{48,496},{56,5... | collective-permute-start | bytes 1474568 | tf_op jit(solution)/shard_map/ppermute | solution.py:23
  70.9 4.0 %collective-permute-done.12.rest_4_ = bf16[384,640]{1,0:T(8,128)(2,1)} collective-permute-done((bf16[384,640]{1,0:T(8,128)(2,1)S(1)}, bf16[384,640]{1,0:T(8,128)(2,1)}, u32[]{:S(2)}, u32[]{:S(2)}) %collective-permute-start.12) | collective-permute-done | bytes 491552 | tf_op jit(solution)/shard_map/ppermute | solution.py:23
  75.0 1.9 %collective-permute-start.13 = (bf16[384,640]{1,0:T(8,128)(2,1)}, bf16[384,640]{1,0:T(8,128)(2,1)S(1)}, u32[]{:S(2)}, u32[]{:S(2)}) collective-permute-start(bf16[384,640]{1,0:T(8,128)(2,1)} %collective-permute-done.12.rest_4_), channel_id=1, source_target_pairs={{0,64},{8,72},{16,80},{24,88},{32,96},{40,104},{48,112},{56,120},{... | collective-permute-start | bytes 1474568 | tf_op jit(solution)/shard_map/ppermute | solution.py:23
  76.9 0.2 and_reduce_fusion
  77.1 4.6 %collective-permute-start.10 = (bf16[384,640]{1,0:T(8,128)(2,1)}, bf16[384,640]{1,0:T(8,128)(2,1)S(1)}, u32[]{:S(2)}, u32[]{:S(2)}) collective-permute-start(bf16[384,640]{1,0:T(8,128)(2,1)} %collective-permute-done.9.rest_1_), channel_id=1, source_target_pairs={{0,448},{8,456},{16,464},{24,472},{32,480},{40,488},{48,496},{56,5... | collective-permute-start | bytes 1474568 | tf_op jit(solution)/shard_map/ppermute | solution.py:23
  81.7 0.1 fusion.4
  81.8 0.1 copy.17
  81.9 0.1 copy.15
  82.0 0.1 div.22
  82.0 0.1 copy.14
  82.2 0.1 and.55
  82.3 3.1 %collective-permute-done.5.rest_3_ = bf16[384,640]{1,0:T(8,128)(2,1)S(1)} collective-permute-done((bf16[384,640]{1,0:T(8,128)(2,1)}, bf16[384,640]{1,0:T(8,128)(2,1)S(1)}, u32[]{:S(2)}, u32[]{:S(2)}) %collective-permute-start.5) | collective-permute-done | bytes 491552 | tf_op jit(solution)/shard_map/ppermute | solution.py:23
  85.4 0.8 slice.27
  86.1 1.9 %collective-permute-start.6 = (bf16[192,640]{1,0:T(8,128)(2,1)}, bf16[192,640]{1,0:T(8,128)(2,1)}, u32[]{:S(2)}, u32[]{:S(2)}) collective-permute-start(bf16[192,640]{1,0:T(8,128)(2,1)} %slice.27), channel_id=1, source_target_pairs={{0,64},{8,72},{16,80},{24,88},{32,96},{40,104},{48,112},{56,120},{... | collective-permute-start | bytes 737288 | tf_op jit(solution)/shard_map/ppermute | solution.py:23
  88.1 0.8 slice.28
  88.8 4.6 %collective-permute-start.7 = (bf16[192,640]{1,0:T(8,128)(2,1)}, bf16[192,640]{1,0:T(8,128)(2,1)}, u32[]{:S(2)}, u32[]{:S(2)}) collective-permute-start(bf16[192,640]{1,0:T(8,128)(2,1)} %slice.28), channel_id=1, source_target_pairs={{0,448},{8,456},{16,464},{24,472},{32,480},{40,488},{48,496},{56,5... | collective-permute-start | bytes 737288 | tf_op jit(solution)/shard_map/ppermute | solution.py:23
  93.4 2.5 %collective-permute-done.13.rest_3_ = bf16[384,640]{1,0:T(8,128)(2,1)S(1)} collective-permute-done((bf16[384,640]{1,0:T(8,128)(2,1)}, bf16[384,640]{1,0:T(8,128)(2,1)S(1)}, u32[]{:S(2)}, u32[]{:S(2)}) %collective-permute-start.13) | collective-permute-done | bytes 491552 | tf_op jit(solution)/shard_map/ppermute | solution.py:23
  95.9 0.8 slice.29
  96.7 1.9 %collective-permute-start.14 = (bf16[224,640]{1,0:T(8,128)(2,1)}, bf16[224,640]{1,0:T(8,128)(2,1)}, u32[]{:S(2)}, u32[]{:S(2)}) collective-permute-start(bf16[224,640]{1,0:T(8,128)(2,1)} %slice.29), channel_id=1, source_target_pairs={{0,64},{8,72},{16,80},{24,88},{32,96},{40,104},{48,112},{56,120},{... | collective-permute-start | bytes 860168 | tf_op jit(solution)/shard_map/ppermute | solution.py:23
  98.6 0.1 fusion.3
  98.7 0.8 slice.30
  99.5 4.6 %collective-permute-start.15 = (bf16[160,640]{1,0:T(8,128)(2,1)}, bf16[160,640]{1,0:T(8,128)(2,1)}, u32[]{:S(2)}, u32[]{:S(2)}) collective-permute-start(bf16[160,640]{1,0:T(8,128)(2,1)} %slice.30), channel_id=1, source_target_pairs={{0,448},{8,456},{16,464},{24,472},{32,480},{40,488},{48,496},{56,5... | collective-permute-start | bytes 614408 | tf_op jit(solution)/shard_map/ppermute | solution.py:23
  104.0 0.1 fusion.1
  104.2 4.8 %scores.1 = (bf16[5,384,384]{2,1,0:T(8,128)(2,1)S(1)}, bf16[15,128,384]{2,1,0:T(8,128)(2,1)S(1)}, f32[3,128,128]{2,1,0:T(8,128)S(1)}) custom-call(s32[27]{0:T(128)S(1)} %pad_add_fusion.table, bf16[384,640]{1,0:T(8,128)(2,1)S(1)} %bitcast.41, bf16[384,640]{1,0:T(8,128)(2,1)S(1)} %bitcast.40, bf16[384,640]{1,0:T(8,128)(2,1)} %copy-done.7, ...), custom_call_target="tpu_custom_call" | custom-call | flops 377487360 | bytes 6291456 | tf_op jit(solution)/shard_map/scores/pallas_call | solution.py:233
  109.1 2.6 %weighted_values.1 = bf16[384,640]{1,0:T(8,128)(2,1)S(1)} custom-call(s32[27]{0:T(128)S(1)} %pad_add_fusion.table, bf16[5,384,384]{2,1,0:T(8,128)(2,1)S(1)} %get-tuple-element.8.near_ref, bf16[15,128,384]{2,1,0:T(8,128)(2,1)S(1)} %get-tuple-element.9.far_ref, f32[3,128,128]{2,1,0:T(8,128)S(1)} %get-tuple-element.10.total_ref, bf16[384,640]{1,0:T(8,128)(2,1)S(1)} %bitcast.44, ...), custom_call_target="tpu_custom_call" | custom-call | flops 377487360 | bytes 6291456 | tf_op jit(solution)/shard_map/weighted_values/pallas_call | solution.py:234
  111.7 15.6 %all_to_all.20 = bf16[8,48,640]{2,1,0:T(8,128)(2,1)S(1)} all-to-all(bf16[8,48,640]{2,1,0:T(8,128)(2,1)S(1)} %bitcast.45), channel_id=1, replica_groups=mesh['seq'=64,'head'=8] {'head'}, dimensions={0} | all-to-all | bytes 983040 | tf_op jit(solution)/shard_map/all_to_all | solution.py:38
  127.3 0.8 copy.25
  (42 shorter events, 0.2 us)
Async XLA Ops:
  0.0 12.3 %copy-start.4 = (bf16[48,5120]{1,0:T(8,128)(2,1)S(1)}, bf16[48,5120]{1,0:T(8,128)(2,1)}, u32[]{:S(2)}) copy-start(bf16[48,5120]{1,0:T(8,128)(2,1)} %param.7) | copy-start | bytes 1474564
  1.9 41.2 %copy-start.5 = (bf16[48,5120]{1,0:T(8,128)(2,1)S(1)}, bf16[48,5120]{1,0:T(8,128)(2,1)}, u32[]{:S(2)}) copy-start(bf16[48,5120]{1,0:T(8,128)(2,1)} %param.5) | copy-start | bytes 1474564
  1.9 19.5 %all-to-all-start.1 = ((bf16[8,48,640]{2,1,0:T(8,128)(2,1)}), bf16[8,48,640]{2,1,0:T(8,128)(2,1)S(1)}, u32[]{:S(2)}, u32[]{:S(2)}) async-start(bf16[8,48,640]{2,1,0:T(8,128)(2,1)} %bitcast.35), calls=%async_computation.1 | async-start | bytes 983040 | tf_op jit(solution)/shard_map/all_to_all | solution.py:30
  21.5 27.0 %copy-start.10 = (s32[24,2]{0,1:T(2,128)S(1)}, s32[24,2]{0,1:T(2,128)}, u32[]{:S(2)}) copy-start(s32[24,2]{0,1:T(2,128)} %param.9) | copy-start | bytes 580
  21.5 35.5 %copy-start.9 = (s32[192,3]{0,1:T(4,128)S(1)}, s32[192,3]{0,1:T(4,128)}, u32[]{:S(2)}) copy-start(s32[192,3]{0,1:T(4,128)} %param.8) | copy-start | bytes 6916
  21.5 13.5 %all-to-all-start.2 = ((bf16[8,48,640]{2,1,0:T(8,128)(2,1)}), bf16[8,48,640]{2,1,0:T(8,128)(2,1)S(1)}, u32[]{:S(2)}, u32[]{:S(2)}) async-start(bf16[8,48,640]{2,1,0:T(8,128)(2,1)} %bitcast.33), calls=%async_computation.2 | async-start | bytes 983040 | tf_op jit(solution)/shard_map/all_to_all | solution.py:30
  25.8 22.6 %collective-permute-start.3 = (bf16[384,640]{1,0:T(8,128)(2,1)S(1)}, bf16[384,640]{1,0:T(8,128)(2,1)S(1)}, u32[]{:S(2)}, u32[]{:S(2)}) collective-permute-start(bf16[384,640]{1,0:T(8,128)(2,1)S(1)} %bitcast.38), channel_id=1, source_target_pairs={{0,64},{8,72},{16,80},{24,88},{32,96},{40,104},{48,112},{56,120},{... | collective-permute-start | bytes 1474568 | tf_op jit(solution)/shard_map/ppermute | solution.py:23
  27.8 22.7 %collective-permute-start = (bf16[384,640]{1,0:T(8,128)(2,1)S(1)}, bf16[384,640]{1,0:T(8,128)(2,1)S(1)}, u32[]{:S(2)}, u32[]{:S(2)}) collective-permute-start(bf16[384,640]{1,0:T(8,128)(2,1)S(1)} %bitcast.39), channel_id=1, source_target_pairs={{0,448},{8,456},{16,464},{24,472},{32,480},{40,488},{48,496},{56,5... | collective-permute-start | bytes 1474568 | tf_op jit(solution)/shard_map/ppermute | solution.py:23
  35.0 20.0 %collective-permute-start.11 = (bf16[384,640]{1,0:T(8,128)(2,1)S(1)}, bf16[384,640]{1,0:T(8,128)(2,1)S(1)}, u32[]{:S(2)}, u32[]{:S(2)}) collective-permute-start(bf16[384,640]{1,0:T(8,128)(2,1)S(1)} %bitcast.42), channel_id=1, source_target_pairs={{0,64},{8,72},{16,80},{24,88},{32,96},{40,104},{48,112},{56,120},{... | collective-permute-start | bytes 1474568 | tf_op jit(solution)/shard_map/ppermute | solution.py:23
  36.9 20.4 %collective-permute-start.8 = (bf16[384,640]{1,0:T(8,128)(2,1)S(1)}, bf16[384,640]{1,0:T(8,128)(2,1)}, u32[]{:S(2)}, u32[]{:S(2)}) collective-permute-start(bf16[384,640]{1,0:T(8,128)(2,1)S(1)} %bitcast.43), channel_id=1, source_target_pairs={{0,448},{8,456},{16,464},{24,472},{32,480},{40,488},{48,496},{56,5... | collective-permute-start | bytes 1474568 | tf_op jit(solution)/shard_map/ppermute | solution.py:23
  43.9 60.3 %all-to-all-start = ((bf16[8,48,640]{2,1,0:T(8,128)(2,1)}), bf16[8,48,640]{2,1,0:T(8,128)(2,1)S(1)}, u32[]{:S(2)}, u32[]{:S(2)}) async-start(bf16[8,48,640]{2,1,0:T(8,128)(2,1)} %bitcast.37), calls=%async_computation | async-start | bytes 983040 | tf_op jit(solution)/shard_map/all_to_all | solution.py:30
  48.5 13.4 %copy-start.6 = (bf16[384,640]{1,0:T(8,128)(2,1)}, bf16[384,640]{1,0:T(8,128)(2,1)S(1)}, u32[]{:S(2)}) copy-start(bf16[384,640]{1,0:T(8,128)(2,1)S(1)} %collective-permute-done.3.rest_5_) | copy-start | bytes 1474564
  48.5 15.9 %collective-permute-start.4 = (bf16[384,640]{1,0:T(8,128)(2,1)S(1)}, bf16[384,640]{1,0:T(8,128)(2,1)}, u32[]{:S(2)}, u32[]{:S(2)}) collective-permute-start(bf16[384,640]{1,0:T(8,128)(2,1)S(1)} %collective-permute-done.3.rest_5_), channel_id=1, source_target_pairs={{0,64},{8,72},{16,80},{24,88},{32,96},{40,104},{48,112},{56,120},{... | collective-permute-start | bytes 1474568 | tf_op jit(solution)/shard_map/ppermute | solution.py:23
  50.4 15.9 %copy-start.7 = (bf16[384,640]{1,0:T(8,128)(2,1)}, bf16[384,640]{1,0:T(8,128)(2,1)S(1)}, u32[]{:S(2)}) copy-start(bf16[384,640]{1,0:T(8,128)(2,1)S(1)} %collective-permute-done.rest_0_) | copy-start | bytes 1474564
  50.5 15.9 %collective-permute-start.1 = (bf16[384,640]{1,0:T(8,128)(2,1)S(1)}, bf16[384,640]{1,0:T(8,128)(2,1)}, u32[]{:S(2)}, u32[]{:S(2)}) collective-permute-start(bf16[384,640]{1,0:T(8,128)(2,1)S(1)} %collective-permute-done.rest_0_), channel_id=1, source_target_pairs={{0,448},{8,456},{16,464},{24,472},{32,480},{40,488},{48,496},{56,5... | collective-permute-start | bytes 1474568 | tf_op jit(solution)/shard_map/ppermute | solution.py:23
  55.1 22.0 %copy-start.8 = (bf16[384,640]{1,0:T(8,128)(2,1)}, bf16[384,640]{1,0:T(8,128)(2,1)S(1)}, u32[]{:S(2)}) copy-start(bf16[384,640]{1,0:T(8,128)(2,1)S(1)} %collective-permute-done.11.rest_5_) | copy-start | bytes 1474564
  55.1 19.9 %collective-permute-start.12 = (bf16[384,640]{1,0:T(8,128)(2,1)S(1)}, bf16[384,640]{1,0:T(8,128)(2,1)}, u32[]{:S(2)}, u32[]{:S(2)}) collective-permute-start(bf16[384,640]{1,0:T(8,128)(2,1)S(1)} %collective-permute-done.11.rest_5_), channel_id=1, source_target_pairs={{0,64},{8,72},{16,80},{24,88},{32,96},{40,104},{48,112},{56,120},{... | collective-permute-start | bytes 1474568 | tf_op jit(solution)/shard_map/ppermute | solution.py:23
  57.3 19.8 %collective-permute-start.9 = (bf16[384,640]{1,0:T(8,128)(2,1)}, bf16[384,640]{1,0:T(8,128)(2,1)}, u32[]{:S(2)}, u32[]{:S(2)}) collective-permute-start(bf16[384,640]{1,0:T(8,128)(2,1)} %collective-permute-done.8.rest_0_), channel_id=1, source_target_pairs={{0,448},{8,456},{16,464},{24,472},{32,480},{40,488},{48,496},{56,5... | collective-permute-start | bytes 1474568 | tf_op jit(solution)/shard_map/ppermute | solution.py:23
  64.4 21.0 %collective-permute-start.5 = (bf16[384,640]{1,0:T(8,128)(2,1)}, bf16[384,640]{1,0:T(8,128)(2,1)S(1)}, u32[]{:S(2)}, u32[]{:S(2)}) collective-permute-start(bf16[384,640]{1,0:T(8,128)(2,1)} %collective-permute-done.4.rest_4_), channel_id=1, source_target_pairs={{0,64},{8,72},{16,80},{24,88},{32,96},{40,104},{48,112},{56,120},{... | collective-permute-start | bytes 1474568 | tf_op jit(solution)/shard_map/ppermute | solution.py:23
  66.4 21.7 %collective-permute-start.2 = (bf16[384,640]{1,0:T(8,128)(2,1)}, bf16[384,640]{1,0:T(8,128)(2,1)S(1)}, u32[]{:S(2)}, u32[]{:S(2)}) collective-permute-start(bf16[384,640]{1,0:T(8,128)(2,1)} %collective-permute-done.1.rest_1_), channel_id=1, source_target_pairs={{0,448},{8,456},{16,464},{24,472},{32,480},{40,488},{48,496},{56,5... | collective-permute-start | bytes 1474568 | tf_op jit(solution)/shard_map/ppermute | solution.py:23
  75.0 21.0 %collective-permute-start.13 = (bf16[384,640]{1,0:T(8,128)(2,1)}, bf16[384,640]{1,0:T(8,128)(2,1)S(1)}, u32[]{:S(2)}, u32[]{:S(2)}) collective-permute-start(bf16[384,640]{1,0:T(8,128)(2,1)} %collective-permute-done.12.rest_4_), channel_id=1, source_target_pairs={{0,64},{8,72},{16,80},{24,88},{32,96},{40,104},{48,112},{56,120},{... | collective-permute-start | bytes 1474568 | tf_op jit(solution)/shard_map/ppermute | solution.py:23
  77.1 21.6 %collective-permute-start.10 = (bf16[384,640]{1,0:T(8,128)(2,1)}, bf16[384,640]{1,0:T(8,128)(2,1)S(1)}, u32[]{:S(2)}, u32[]{:S(2)}) collective-permute-start(bf16[384,640]{1,0:T(8,128)(2,1)} %collective-permute-done.9.rest_1_), channel_id=1, source_target_pairs={{0,448},{8,456},{16,464},{24,472},{32,480},{40,488},{48,496},{56,5... | collective-permute-start | bytes 1474568 | tf_op jit(solution)/shard_map/ppermute | solution.py:23
  85.4 18.8 %copy-start.1 = (bf16[384,640]{1,0:T(8,128)(2,1)}, bf16[384,640]{1,0:T(8,128)(2,1)S(1)}, u32[]{:S(2)}) copy-start(bf16[384,640]{1,0:T(8,128)(2,1)S(1)} %collective-permute-done.5.rest_3_) | copy-start | bytes 1474564
  86.1 18.1 %collective-permute-start.6 = (bf16[192,640]{1,0:T(8,128)(2,1)}, bf16[192,640]{1,0:T(8,128)(2,1)}, u32[]{:S(2)}, u32[]{:S(2)}) collective-permute-start(bf16[192,640]{1,0:T(8,128)(2,1)} %slice.27), channel_id=1, source_target_pairs={{0,64},{8,72},{16,80},{24,88},{32,96},{40,104},{48,112},{56,120},{... | collective-permute-start | bytes 737288 | tf_op jit(solution)/shard_map/ppermute | solution.py:23
  88.1 16.2 %copy-start.2 = (bf16[384,640]{1,0:T(8,128)(2,1)}, bf16[384,640]{1,0:T(8,128)(2,1)S(1)}, u32[]{:S(2)}) copy-start(bf16[384,640]{1,0:T(8,128)(2,1)S(1)} %collective-permute-done.2.rest_2_) | copy-start | bytes 1474564
  88.8 15.4 %collective-permute-start.7 = (bf16[192,640]{1,0:T(8,128)(2,1)}, bf16[192,640]{1,0:T(8,128)(2,1)}, u32[]{:S(2)}, u32[]{:S(2)}) collective-permute-start(bf16[192,640]{1,0:T(8,128)(2,1)} %slice.28), channel_id=1, source_target_pairs={{0,448},{8,456},{16,464},{24,472},{32,480},{40,488},{48,496},{56,5... | collective-permute-start | bytes 737288 | tf_op jit(solution)/shard_map/ppermute | solution.py:23
  95.9 13.1 %copy-start = (bf16[384,640]{1,0:T(8,128)(2,1)}, bf16[384,640]{1,0:T(8,128)(2,1)S(1)}, u32[]{:S(2)}) copy-start(bf16[384,640]{1,0:T(8,128)(2,1)S(1)} %collective-permute-done.13.rest_3_) | copy-start | bytes 1474564
  96.7 12.4 %collective-permute-start.14 = (bf16[224,640]{1,0:T(8,128)(2,1)}, bf16[224,640]{1,0:T(8,128)(2,1)}, u32[]{:S(2)}, u32[]{:S(2)}) collective-permute-start(bf16[224,640]{1,0:T(8,128)(2,1)} %slice.29), channel_id=1, source_target_pairs={{0,64},{8,72},{16,80},{24,88},{32,96},{40,104},{48,112},{56,120},{... | collective-permute-start | bytes 860168 | tf_op jit(solution)/shard_map/ppermute | solution.py:23
  98.7 10.4 %copy-start.3 = (bf16[384,640]{1,0:T(8,128)(2,1)}, bf16[384,640]{1,0:T(8,128)(2,1)S(1)}, u32[]{:S(2)}) copy-start(bf16[384,640]{1,0:T(8,128)(2,1)S(1)} %collective-permute-done.10.rest_2_) | copy-start | bytes 1474564
  99.5 9.6 %collective-permute-start.15 = (bf16[160,640]{1,0:T(8,128)(2,1)}, bf16[160,640]{1,0:T(8,128)(2,1)}, u32[]{:S(2)}, u32[]{:S(2)}) collective-permute-start(bf16[160,640]{1,0:T(8,128)(2,1)} %slice.30), channel_id=1, source_target_pairs={{0,448},{8,456},{16,464},{24,472},{32,480},{40,488},{48,496},{56,5... | collective-permute-start | bytes 614408 | tf_op jit(solution)/shard_map/ppermute | solution.py:23
